TPU v7x, 512 devices: a whole 4x4x16 slice. The times are simulated.
512 devices in a mesh: section: 16 (over x_lo, y, core), expert: 32 (over x_hi, z).
Axes of the slice: x: 4 (x_hi: 2, x_lo: 2; x = x_hi * 2 + x_lo), y: 4, z: 16, core: 2. Of those that a mesh axis runs over, the one named last changes fastest.
Arguments:
- tokens: bfloat16 [4608, 3584], P('expert', 'section'), may hold values from -6 to 6
- norm_gain: bfloat16 [1, 3584], P(None, 'section'), may hold values from 0.5 to 1.5
- expert_ids: int32 [4608, 2], P('expert'), may hold values from 0 to 31, all different within a row; in each aligned block of 144 rows (0 to 143, 144 to 287, ...) at most 18 rows name the same one
- gate_weight: float32 [4608, 2], P('expert'), may hold values from 0.2 to 1
- w_gate: bfloat16 [32, 3584, 2048], P('expert', None, 'section'), may hold values from -0.09375 to 0.09375
- w_up: bfloat16 [32, 3584, 2048], P('expert', None, 'section'), may hold values from -0.09375 to 0.09375
- w_down: bfloat16 [32, 2048, 3584], P('expert', 'section'), may hold values from -0.125 to 0.125
Outputs:
- mixed_out: bfloat16 [4608, 3584], P('expert', 'section')
Inputs may be any that keep to these rules, and one draw needn't show every extreme that they name: `expert_ids`: each token names 2 different experts; among the 144 tokens of one index of the expert axis no expert is named more than 18 times, a bound that some block reaches.
All inputs are finite; a program needn't handle non-finite values.
Results may differ from a plain program's by a relative error of at most 0.023.
Values may be sent and summed in bfloat16 or wider, within the bound.
A program may use at most 128 MiB of HBM per device.

v0:
```python
import jax
import jax.numpy as jnp
from jax import lax
from jax.sharding import PartitionSpec as P

epsilon = 1e-06


def slot_table(expert_ids, experts, capacity):
    token_count, routes = expert_ids.shape
    flat_ids = expert_ids.reshape(-1)
    onehot = (flat_ids[:, None] == jnp.arange(experts, dtype=jnp.int32)[None, :]).astype(jnp.int32)
    before = jnp.cumsum(onehot, axis=0) - onehot
    slot = jnp.sum(before * onehot, axis=1)
    return (flat_ids * capacity + slot).reshape(token_count, routes)


def on_device(tokens, norm_gain, expert_ids, gate_weight, w_gate, w_up, w_down):
    experts = lax.axis_size("expert")
    token_count, routes = expert_ids.shape
    capacity = 2 * token_count * routes // experts
    model_width = w_gate.shape[1]
    position = slot_table(expert_ids, experts, capacity)
    places = jnp.arange(experts * capacity, dtype=jnp.int32)
    dispatch_map = jnp.sum(
        (places[:, None, None] == position[None, :, :]).astype(jnp.int32), axis=2
    ).astype(jnp.bfloat16)
    gate_matrix = w_gate[0]
    up_matrix = w_up[0]
    gathered, gain_full = (
        lax.all_gather(tokens, "section", axis=1, tiled=True),
        lax.all_gather(norm_gain, "section", axis=1, tiled=True),
    )
    floats = gathered.astype(jnp.float32)
    mean_square = jnp.mean(floats * floats, axis=1, keepdims=True)
    normed = (floats * lax.rsqrt(mean_square + epsilon) * gain_full.astype(jnp.float32)).astype(
        jnp.bfloat16
    )
    buffer = jnp.dot(dispatch_map, normed, preferred_element_type=jnp.float32).astype(jnp.bfloat16)
    buffer = buffer.reshape(experts, capacity, model_width)
    arrived = lax.all_to_all(buffer, "expert", split_axis=0, concat_axis=0, tiled=True).reshape(
        experts * capacity, model_width
    )
    gate_pre = jnp.dot(arrived, gate_matrix, preferred_element_type=jnp.float32)
    up_pre = jnp.dot(arrived, up_matrix, preferred_element_type=jnp.float32)
    hidden = (jax.nn.silu(gate_pre) * up_pre).astype(jnp.bfloat16)
    partial_value = jnp.dot(hidden, w_down[0], preferred_element_type=jnp.float32)
    rounded = lax.optimization_barrier(partial_value.astype(jnp.bfloat16))
    summed = lax.psum_scatter(
        rounded.astype(jnp.float32).astype(jnp.bfloat16), "section", scatter_dimension=1, tiled=True
    ).astype(jnp.float32)
    returned_rows = lax.all_to_all(
        summed.reshape(experts, capacity, summed.shape[1]).astype(jnp.bfloat16),
        "expert",
        split_axis=0,
        concat_axis=0,
        tiled=True,
    ).astype(jnp.float32)
    returned_rows = returned_rows.reshape(experts * capacity, summed.shape[1])
    picked = returned_rows[position]
    mixed_out = jnp.sum(gate_weight[:, :, None] * picked, axis=1).astype(jnp.bfloat16)
    return mixed_out


def solution(mesh):
    placed = (
        P("expert", "section"),
        P(None, "section"),
        P("expert", None),
        P("expert", None),
        P("expert", None, "section"),
        P("expert", None, "section"),
        P("expert", "section", None),
    )
    return jax.shard_map(
        on_device, mesh=mesh, in_specs=placed, out_specs=P("expert", "section"), check_vma=False
    )
```

profile of v0, /device:TPU:6, one launch (start us, length us, event | category | flops | bytes accessed | tf_op | source)
XLA Modules:
  0.0 482.8 jit_solution(3069950790144365907)
XLA Ops:
  6.5 0.0 copy-start
  6.5 0.0 reduce-scatter.4.cloned.1.call-start
  6.5 0.9 copy.33
  7.4 0.1 eq.36
  7.6 0.9 reduce-window.6
  8.5 0.2 slice_reduce_fusion
  8.7 0.1 bitcast_bitcast_fusion
  8.8 0.1 reduce_sum.39
  9.0 0.1 copy.36
  9.1 0.7 compare_select_fusion
  9.8 0.1 convert_reduce_fusion
  9.9 22.8 %all-gather = bf16[16,224,144]{1,2,0:T(8,128)(2,1)S(1)} all-gather(bf16[1,224,144]{1,2,0:T(8,128)(2,1)} %bitcast.35), channel_id=1, replica_groups=mesh['section'=16,'expert'=32] {'section'}, dimensions={0}, use_global_device_ids=true | all-gather | bytes 1096704 | tf_op jit(solution)/shard_map/all_gather | solution.py:31
  32.7 1.8 copy.37
  34.5 0.0 copy-start.3
  34.5 2.7 reshape.73
  37.3 0.2 multiply_reduce_fusion
  37.5 1.3 dynamic-slice
  39.4 0.0 copy-done.3
  39.5 0.2 dynamic-update-slice
  39.7 28.0 %all-reduce.1 = bf16[3584]{0:T(1024)(128)(2,1)S(1)} all-reduce(bf16[3584]{0:T(1024)(128)(2,1)S(1)} %dynamic-update-slice), channel_id=1, replica_groups=mesh['section'=16,'expert'=32] {'section'}, use_global_device_ids=true, to_apply=%add.1 | all-reduce | flops 3584 | bytes 14336
  67.8 3.3 convolution_convert_fusion
  71.1 7.2 %reshape.46 = bf16[32,18,3584]{2,1,0:T(8,128)(2,1)} reshape(bf16[576,3584]{1,0:T(8,128)(2,1)} %convolution_convert_fusion) | data formatting | bytes 8257536 | tf_op jit(solution)/shard_map/reshape | solution.py:40
  78.3 264.0 %all_to_all.10 = bf16[32,18,3584]{2,1,0:T(8,128)(2,1)} all-to-all(bf16[32,18,3584]{2,1,0:T(8,128)(2,1)} %reshape.46), channel_id=1, replica_groups=mesh['section'=16,'expert'=32] {'expert'}, dimensions={0} | all-to-all | bytes 8257536 | tf_op jit(solution)/shard_map/all_to_all | solution.py:41
  342.4 0.0 copy-start.4
  342.4 7.4 %reshape.47 = bf16[576,3584]{1,0:T(8,128)(2,1)} reshape(bf16[32,18,3584]{2,1,0:T(8,128)(2,1)} %all_to_all.10) | data formatting | bytes 8257536 | tf_op jit(solution)/shard_map/reshape | solution.py:41
  349.8 0.0 copy-done.4
  349.8 0.0 copy-start.1
  349.8 3.5 fusion.6
  353.3 0.0 copy-done
  353.3 0.0 copy-done.1
  353.3 8.5 %convolution_convert_fusion.1 = bf16[576,3584]{1,0:T(8,128)(2,1)} fusion(bf16[576,3584]{1,0:T(8,128)(2,1)} %reshape.47, bf16[1,128,3584]{2,1,0:T(8,128)(2,1)S(1)} %copy-done, bf16[1,3584,128]{2,1,0:T(8,128)(2,1)S(1)} %copy-done.1, f32[576,128]{1,0:T(8,128)S(1)} %fusion.6), kind=kOutput, calls=%fused_computation.2 | convolution fusion | flops 1059471360 | bytes 10387456 | tf_op jit(solution)/shard_map/dot_general | solution.py:47
  361.8 6.5 %copy.39 = bf16[576,3584]{0,1:T(8,128)(2,1)} copy(bf16[576,3584]{1,0:T(8,128)(2,1)} %convolution_convert_fusion.1) | data formatting | bytes 8257536
  368.3 0.0 copy-start.2
  368.3 0.0 reduce-scatter.4.cloned.1.call-update
  368.3 63.9 %reduce-scatter.4.cloned.1.call-done = bf16[224,576]{1,0:T(8,128)(2,1)} async-done(((bf16[3584,576]{1,0:T(8,128)(2,1)}), bf16[224,576]{1,0:T(8,128)(2,1)}) %reduce-scatter.4.cloned.1.call-update) | async-done | bytes 258064
  432.2 1.1 copy.40
  433.3 0.8 convert_element_type.45
  434.2 15.5 %all-to-all-start.1 = ((bf16[32,18,224]{2,1,0:T(8,128)(2,1)}), bf16[32,18,224]{2,1,0:T(8,128)(2,1)S(1)}, u32[]{:S(2)}, u32[]{:S(2)}) async-start(bf16[32,18,224]{2,1,0:T(8,128)(2,1)} %convert_element_type.45), calls=%async_computation.1 | async-start | bytes 786432 | tf_op jit(solution)/shard_map/all_to_all | solution.py:52
  449.7 0.1 copy.38
  449.8 0.1 reshape.56
  450.0 0.0 copy-done.2
  450.0 0.1 copy.32
  450.1 22.9 %all-to-all-done.1 = bf16[32,18,224]{2,1,0:T(8,128)(2,1)S(1)} async-done(((bf16[32,18,224]{2,1,0:T(8,128)(2,1)}), bf16[32,18,224]{2,1,0:T(8,128)(2,1)S(1)}, u32[]{:S(2)}, u32[]{:S(2)}) %all-to-all-start.1) | async-done | bytes 258080 | tf_op jit(solution)/shard_map/all_to_all | solution.py:52
  473.0 0.1 reshape.53
  473.1 1.6 gather_fusion
  474.7 0.2 reshape.55
  474.9 1.1 multiply_reduce_fusion.1
  (9 shorter events, 0.1 us)
Async XLA Ops:
  6.5 346.7 %copy-start = (bf16[1,128,3584]{2,1,0:T(8,128)(2,1)S(1)}, bf16[1,128,3584]{2,1,0:T(8,128)(2,1)}, u32[]{:S(2)}) copy-start(bf16[1,128,3584]{2,1,0:T(8,128)(2,1)} %param.13) | copy-start | bytes 2752516
  6.5 425.7 %reduce-scatter.4.cloned.1.call-start = ((), (), s32[]{:S(2)}) async-start(), calls=%async_computation.3 | async-start | bytes 4874240
  34.5 4.9 %copy-start.3 = (bf16[1,224]{1,0:T(2,128)(2,1)S(1)}, bf16[1,224]{1,0:T(2,128)(2,1)}, u32[]{:S(2)}) copy-start(bf16[1,224]{1,0:T(2,128)(2,1)} %param.8) | copy-start | bytes 1348
  342.4 7.4 %copy-start.4 = (bf16[1,3584,128]{2,1,0:T(8,128)(2,1)S(1)}, bf16[1,3584,128]{2,1,0:T(8,128)(2,1)}, u32[]{:S(2)}) copy-start(bf16[1,3584,128]{2,1,0:T(8,128)(2,1)} %param.11) | copy-start | bytes 2752516
  349.8 3.5 copy-start.1
  368.3 81.7 %copy-start.2 = (f32[144,2]{0,1:T(2,128)S(1)}, f32[144,2]{0,1:T(2,128)}, u32[]{:S(2)}) copy-start(f32[144,2]{0,1:T(2,128)} %param.10) | copy-start | bytes 3460
  434.2 38.8 %all-to-all-start.1 = ((bf16[32,18,224]{2,1,0:T(8,128)(2,1)}), bf16[32,18,224]{2,1,0:T(8,128)(2,1)S(1)}, u32[]{:S(2)}, u32[]{:S(2)}) async-start(bf16[32,18,224]{2,1,0:T(8,128)(2,1)} %convert_element_type.45), calls=%async_computation.1 | async-start | bytes 786432 | tf_op jit(solution)/shard_map/all_to_all | solution.py:52
Sparse Core Ops, SparseCore 0:
  368.4 63.7 reduce-scatter.3
where the time goes:
time: 486 us; the launch traced here: 483 us
  blocking collectives  315 us (65%)
  waiting for transfers between devices  86.7 us (18%)
  local copies, waits for them, and re-layouts  32.8 us (7%)
  starting transfers between devices  15.5 us (3%)
  matrix products  15.3 us (3%)
  between operations  14.2 us (3%)
    all_to_all x1, blocking collectives, on_device(): lax.all_to_all(buffer, 'expert', split_axis=0, concat_axis=0, tiled=True)  264 us
    unnamed x2, waiting for transfers between devices  63.9 us
    unnamed x1, blocking collectives  28 us
    all_to_all x1, waiting for transfers between devices, on_device(): lax.all_to_all(summed.reshape(experts, capacity, summed.shape[1]).astype(...  22.9 us
    all_gather x1, blocking collectives, on_device(): lax.all_gather(tokens, 'section', axis=1, tiled=True)  22.8 us
    all_to_all x1, starting transfers between devices, on_device(): lax.all_to_all(summed.reshape(experts, capacity, summed.shape[1]).astype(...  15.5 us
    unnamed x17, local copies, waits for them, and re-layouts  10.1 us
  transfers between devices with their start and end apart: 2, of which 2 were waited for; matrix products, arithmetic and copies ran while one was open for 0% of the time, Pallas kernels for 0%

commit v1 on v0

--- a/solution.py
+++ b/solution.py
@@ -19,7 +19,6 @@
     experts = lax.axis_size("expert")
     token_count, routes = expert_ids.shape
     capacity = 2 * token_count * routes // experts
-    model_width = w_gate.shape[1]
     position = slot_table(expert_ids, experts, capacity)
     places = jnp.arange(experts * capacity, dtype=jnp.int32)
     dispatch_map = jnp.sum(
@@ -27,19 +26,20 @@
     ).astype(jnp.bfloat16)
     gate_matrix = w_gate[0]
     up_matrix = w_up[0]
-    gathered, gain_full = (
-        lax.all_gather(tokens, "section", axis=1, tiled=True),
-        lax.all_gather(norm_gain, "section", axis=1, tiled=True),
+    buffer = jnp.dot(dispatch_map, tokens, preferred_element_type=jnp.float32).astype(jnp.bfloat16)
+    buffer = buffer.reshape(experts, capacity, tokens.shape[1])
+    own_part = lax.all_to_all(buffer, "expert", split_axis=0, concat_axis=0, tiled=True).reshape(
+        experts * capacity, tokens.shape[1]
     )
-    floats = gathered.astype(jnp.float32)
+    with_gain = jnp.concatenate(
+        [own_part, jnp.broadcast_to(norm_gain, (16, norm_gain.shape[1]))], axis=0
+    )
+    gathered = lax.all_gather(with_gain, "section", axis=1, tiled=True)
+    floats = gathered[: experts * capacity].astype(jnp.float32)
+    gain_full = gathered[experts * capacity : experts * capacity + 1]
     mean_square = jnp.mean(floats * floats, axis=1, keepdims=True)
-    normed = (floats * lax.rsqrt(mean_square + epsilon) * gain_full.astype(jnp.float32)).astype(
+    arrived = (floats * lax.rsqrt(mean_square + epsilon) * gain_full.astype(jnp.float32)).astype(
         jnp.bfloat16
-    )
-    buffer = jnp.dot(dispatch_map, normed, preferred_element_type=jnp.float32).astype(jnp.bfloat16)
-    buffer = buffer.reshape(experts, capacity, model_width)
-    arrived = lax.all_to_all(buffer, "expert", split_axis=0, concat_axis=0, tiled=True).reshape(
-        experts * capacity, model_width
     )
     gate_pre = jnp.dot(arrived, gate_matrix, preferred_element_type=jnp.float32)
     up_pre = jnp.dot(arrived, up_matrix, preferred_element_type=jnp.float32)

time: 486 us -> 245 us (0.50)
  blocking collectives: 315 us -> 0 us
  waiting for transfers between devices: 86.7 us -> 161 us
  local copies, waits for them, and re-layouts: 32.8 us -> 14.4 us
  starting transfers between devices: 15.5 us -> 33.6 us
    all_to_all x1 -> x0, blocking collectives: 264 us -> none  [on_device(): lax.all_to_all(buffer, 'expert', split_axis=0, concat_axis=0, tiled=True)]
    all_gather x0 -> x1, waiting for transfers between devices: none -> 37.8 us  [on_device(): gathered = lax.all_gather(with_gain, 'section', axis=1, tiled=True)]
    unnamed x1 -> x0, blocking collectives: 28 us -> none
    all_to_all x0 -> x1, waiting for transfers between devices: none -> 25.5 us  [on_device(): lax.all_to_all(buffer, 'expert', split_axis=0, concat_axis=0, tiled=True)]
    all_gather x1 -> x0, blocking collectives: 22.8 us -> none  [on_device(): lax.all_gather(tokens, 'section', axis=1, tiled=True)]
    all_to_all x0 -> x1, starting transfers between devices: none -> 18.2 us  [on_device(): lax.all_to_all(buffer, 'expert', split_axis=0, concat_axis=0, tiled=True)]
    unnamed x2 -> x3, waiting for transfers between devices: 63.9 us -> 75.1 us
    reshape x1, local copies, waits for them, and re-layouts: 7.4 us -> 0.14 us  [on_device(): lax.all_to_all(buffer, 'expert', split_axis=0, concat_axis=0, tiled=True)]
  transfers between devices with their start and end apart: 2 -> 4, of which waited for: 2 -> 4; matrix products, arithmetic and copies ran while one was open for 0% -> 0% of each run, Pallas kernels for 0% -> 0%
where the time goes in v1:
time: 245 us; the launch traced here: 243 us
  waiting for transfers between devices  161 us (66%)
  starting transfers between devices  33.6 us (14%)
  local copies, waits for them, and re-layouts  14.4 us (6%)
  between operations  13.6 us (6%)
  matrix products  11.9 us (5%)
  other arithmetic  7.83 us (3%)
    unnamed x3, waiting for transfers between devices  75.1 us
    all_gather x1, waiting for transfers between devices, on_device(): gathered = lax.all_gather(with_gain, 'section', axis=1, tiled=True)  37.8 us
    all_to_all x1, waiting for transfers between devices, on_device(): lax.all_to_all(buffer, 'expert', split_axis=0, concat_axis=0, tiled=True)  25.5 us
    all_to_all x1, waiting for transfers between devices, on_device(): lax.all_to_all(summed.reshape(experts, capacity, summed.shape[1]).astype(...  22.9 us
    all_to_all x1, starting transfers between devices, on_device(): lax.all_to_all(buffer, 'expert', split_axis=0, concat_axis=0, tiled=True)  18.2 us
    all_to_all x1, starting transfers between devices, on_device(): lax.all_to_all(summed.reshape(experts, capacity, summed.shape[1]).astype(...  15.3 us
    dot_general x1, matrix products, on_device(): jnp.dot(hidden, w_down[0], preferred_element_type=jnp.float32)  8.82 us
    unnamed x14, local copies, waits for them, and re-layouts  8.79 us
  transfers between devices with their start and end apart: 4, of which 4 were waited for; matrix products, arithmetic and copies ran while one was open for 0% of the time, Pallas kernels for 0%

profile of v1, /device:TPU:6, one launch (start us, length us, event | category | flops | bytes accessed | tf_op | source)
XLA Modules:
  0.0 242.7 jit_solution(4742288861300260495)
XLA Ops:
  6.5 0.0 copy-start
  6.5 0.9 copy.35
  7.4 0.1 eq.36
  7.6 0.9 reduce-window.6
  8.5 0.2 slice_reduce_fusion
  8.7 0.1 bitcast_bitcast_fusion
  8.8 0.1 reduce_sum.39
  9.0 0.1 copy.38
  9.1 0.7 compare_select_fusion
  9.8 0.1 convert_reduce_fusion.1
  9.9 1.2 convolution_convert_fusion.1
  11.1 0.2 copy.39
  11.3 0.0 copy-start.3
  11.3 0.8 reshape.46
  12.1 18.2 %all-to-all-start = ((bf16[32,18,224]{2,1,0:T(8,128)(2,1)}), bf16[32,18,224]{2,1,0:T(8,128)(2,1)S(1)}, u32[]{:S(2)}, u32[]{:S(2)}) async-start(bf16[32,18,224]{2,1,0:T(8,128)(2,1)} %reshape.46), calls=%async_computation | async-start | bytes 786432 | tf_op jit(solution)/shard_map/all_to_all | solution.py:31
  30.4 0.0 all-gather.2.cloned.1.call-start
  30.4 0.7 reduce.1
  31.1 25.5 %all-to-all-done = bf16[32,18,224]{2,1,0:T(8,128)(2,1)S(1)} async-done(((bf16[32,18,224]{2,1,0:T(8,128)(2,1)}), bf16[32,18,224]{2,1,0:T(8,128)(2,1)S(1)}, u32[]{:S(2)}, u32[]{:S(2)}) %all-to-all-start) | async-done | bytes 258080 | tf_op jit(solution)/shard_map/all_to_all | solution.py:31
  56.6 0.1 reshape.47
  56.8 0.9 copy.40
  57.7 0.0 all-gather.2.cloned.1.call-update
  57.8 0.0 reduce-scatter.4.cloned.1.call-start
  57.8 37.8 %all-gather.2.cloned.1.call-done = bf16[592,3584]{0,1:T(8,128)(2,1)} async-done(((bf16[592,224]{0,1:T(8,128)(2,1)}), bf16[592,3584]{0,1:T(8,128)(2,1)}) %all-gather.2.cloned.1.call-update) | async-done | bytes 4243472 | tf_op jit(solution)/shard_map/all_gather | solution.py:37
  95.6 0.0 copy-start.1
  95.6 3.5 %fusion = f32[576]{0:T(1024)S(1)} fusion(bf16[592,3584]{0,1:T(8,128)(2,1)} %all-gather.2.cloned.1.call-done), kind=kLoop, calls=%fused_computation.3 | loop fusion | flops 6192576 | bytes 4131072 | tf_op jit(solution)/shard_map/reduce_sum | solution.py:40
  99.1 0.2 copy-done.1
  99.3 0.6 convert_reduce_fusion
  99.9 0.0 copy-done.3
  100.0 0.0 copy-start.4
  100.0 1.9 fusion.7
  101.9 0.0 copy-done
  101.9 0.0 copy-done.4
  101.9 8.8 %convolution_convert_fusion = bf16[576,3584]{1,0:T(8,128)(2,1)} fusion(bf16[1,128,3584]{2,1,0:T(8,128)(2,1)S(1)} %copy-done, bf16[1,3584,128]{2,1,0:T(8,128)(2,1)S(1)} %copy-done.4, f32[3584]{0:T(1024)S(1)} %convert_reduce_fusion, f32[576]{0:T(1024)S(1)} %add_rsqrt_fusion, bf16[592,3584]{0,1:T(8,128)(2,1)} %all-gather.2.cloned.1.call-done, ...), kind=kOutput, calls=%fused_computation.6 | convolution fusion | flops 1067728896 | bytes 10518784 | tf_op jit(solution)/shard_map/dot_general | solution.py:47
  110.7 6.5 %copy.42 = bf16[576,3584]{0,1:T(8,128)(2,1)} copy(bf16[576,3584]{1,0:T(8,128)(2,1)} %convolution_convert_fusion) | data formatting | bytes 8257536
  117.2 0.0 reduce-scatter.4.cloned.1.call-update
  117.3 75.1 %reduce-scatter.4.cloned.1.call-done = bf16[224,576]{1,0:T(8,128)(2,1)} async-done(((bf16[3584,576]{1,0:T(8,128)(2,1)}), bf16[224,576]{1,0:T(8,128)(2,1)}) %reduce-scatter.4.cloned.1.call-update) | async-done | bytes 258064
  192.4 1.1 copy.43
  193.5 0.8 convert_element_type.45
  194.3 15.3 %all-to-all-start.1 = ((bf16[32,18,224]{2,1,0:T(8,128)(2,1)}), bf16[32,18,224]{2,1,0:T(8,128)(2,1)S(1)}, u32[]{:S(2)}, u32[]{:S(2)}) async-start(bf16[32,18,224]{2,1,0:T(8,128)(2,1)} %convert_element_type.45), calls=%async_computation.1 | async-start | bytes 786432 | tf_op jit(solution)/shard_map/all_to_all | solution.py:52
  209.6 0.1 copy.41
  209.7 0.1 reshape.56
  209.9 0.0 copy-done.2
  209.9 0.1 copy.34
  210.0 22.9 %all-to-all-done.1 = bf16[32,18,224]{2,1,0:T(8,128)(2,1)S(1)} async-done(((bf16[32,18,224]{2,1,0:T(8,128)(2,1)}), bf16[32,18,224]{2,1,0:T(8,128)(2,1)S(1)}, u32[]{:S(2)}, u32[]{:S(2)}) %all-to-all-start.1) | async-done | bytes 258080 | tf_op jit(solution)/shard_map/all_to_all | solution.py:52
  232.9 0.1 reshape.53
  233.0 1.6 gather_fusion
  234.6 0.2 reshape.55
  234.8 1.1 multiply_reduce_fusion
  (9 shorter events, 0.2 us)
Async XLA Ops:
  6.5 95.4 %copy-start = (bf16[1,128,3584]{2,1,0:T(8,128)(2,1)S(1)}, bf16[1,128,3584]{2,1,0:T(8,128)(2,1)}, u32[]{:S(2)}) copy-start(bf16[1,128,3584]{2,1,0:T(8,128)(2,1)} %param.13) | copy-start | bytes 2752516
  11.3 88.7 %copy-start.3 = (bf16[1,3584,128]{2,1,0:T(8,128)(2,1)S(1)}, bf16[1,3584,128]{2,1,0:T(8,128)(2,1)}, u32[]{:S(2)}) copy-start(bf16[1,3584,128]{2,1,0:T(8,128)(2,1)} %param.11) | copy-start | bytes 2752516
  12.1 44.5 %all-to-all-start = ((bf16[32,18,224]{2,1,0:T(8,128)(2,1)}), bf16[32,18,224]{2,1,0:T(8,128)(2,1)S(1)}, u32[]{:S(2)}, u32[]{:S(2)}) async-start(bf16[32,18,224]{2,1,0:T(8,128)(2,1)} %reshape.46), calls=%async_computation | async-start | bytes 786432 | tf_op jit(solution)/shard_map/all_to_all | solution.py:31
  30.4 65.3 %all-gather.2.cloned.1.call-start = ((), (), s32[]{:S(2)}) async-start(), calls=%async_computation.3 | async-start | bytes 4874240 | tf_op jit(solution)/shard_map/all_gather | solution.py:37
  57.8 134.6 %reduce-scatter.4.cloned.1.call-start = ((), (), s32[]{:S(2)}) async-start(), calls=%async_computation.4 | async-start | bytes 4874240
  95.6 3.7 %copy-start.1 = (bf16[592,3584]{0,1:T(8,128)(2,1)S(1)}, bf16[592,3584]{0,1:T(8,128)(2,1)}, u32[]{:S(2)}) copy-start(bf16[592,3584]{0,1:T(8,128)(2,1)} %all-gather.2.cloned.1.call-done) | copy-start | bytes 12730372
  100.0 2.0 copy-start.4
  117.2 92.6 %copy-start.2 = (f32[144,2]{0,1:T(2,128)S(1)}, f32[144,2]{0,1:T(2,128)}, u32[]{:S(2)}) copy-start(f32[144,2]{0,1:T(2,128)} %param.10) | copy-start | bytes 3460
  194.3 38.5 %all-to-all-start.1 = ((bf16[32,18,224]{2,1,0:T(8,128)(2,1)}), bf16[32,18,224]{2,1,0:T(8,128)(2,1)S(1)}, u32[]{:S(2)}, u32[]{:S(2)}) async-start(bf16[32,18,224]{2,1,0:T(8,128)(2,1)} %convert_element_type.45), calls=%async_computation.1 | async-start | bytes 786432 | tf_op jit(solution)/shard_map/all_to_all | solution.py:52
Sparse Core Ops, SparseCore 0:
  57.9 37.7 all-gather.1
  117.4 74.9 reduce-scatter.3

commit v2 on v1

v2 whole, which is shorter than its diff:
```python
import jax
import jax.numpy as jnp
from jax import lax
from jax.experimental import pallas as pl
from jax.experimental.pallas import tpu as pltpu
from jax.sharding import PartitionSpec as P

epsilon = 1e-06
D = 3584
FEAT = 224
LANES = 256
TOK = 144
SLOTS = 16
GROUPS = 4
PER = 8
MAIN = PER * SLOTS
ROWS = MAIN + 2 * PER
F32 = jnp.float32
BF16 = jnp.bfloat16
I32 = jnp.int32
MESH = pl.DeviceIdType.MESH


def iota(shape, dim):
    return lax.broadcasted_iota(I32, shape, dim)


def one_hot(mask):
    return jnp.where(mask, 1.0, 0.0).astype(BF16)


def dot(a, b):
    return jnp.dot(a, b, preferred_element_type=F32)


def peer_expert(place, xh, z, sign):
    step = place // 2
    half = (step + 1) // 2
    offset = half * (2 * (step % 2) - 1)
    return ((xh + place % 2) % 2) * 16 + (z + sign * offset + 16) % 16


def piece_of(slot):
    return slot - 7 * (slot >= 7).astype(I32)


def unfold(packed):
    rows = packed.shape[0]
    lane = iota((128, LANES), 1)
    spread = one_hot((iota((128, LANES), 0) - 96 == lane % 32) & (lane < FEAT))
    copies = dot(packed[:, 128:256], spread)
    slot = iota((rows, LANES), 0) % 16
    keep = (iota((rows, LANES), 1) // 32 == piece_of(slot)) & (slot < 14)
    return jnp.where(keep, copies, 0.0).astype(BF16)


def fold(spread):
    rows, width = spread.shape
    slot = iota((rows, width), 0) % 16
    keep = (iota((rows, width), 1) // 32 == piece_of(slot)) & (slot < 14)
    own = jnp.where(keep, spread, 0.0).astype(BF16)
    lane = iota((width, LANES), 1)
    gather = one_hot((lane >= FEAT) & (iota((width, LANES), 0) % 32 == lane - FEAT))
    return dot(own, gather)


def kernel(
    tokens, ids, ids_t, gate_weight, gain, w_gate, w_up, w_down, out,
    pack, arrived, blocks, wide, down, down_raw, hidden, core_out, core_in, sums, y_in, x_out, x_in,
    back, returned, picks, total0, total1,
    w_sem, z_send, z_recv, g_send, g_x, g_y, g_core, p_send, p_recv, r_send, r_recv, x_send, x_recv,
    b_send, b_recv,
):
    section, expert = lax.axis_index("section"), lax.axis_index("expert")
    xl, y, core = section // 8, (section // 2) % 4, section % 2
    xh, z = expert // 16, expert % 16
    up, dn, far = (y + 1) % 4, (y + 3) % 4, (y + 2) % 4
    ox = 1 - xl

    def sec(a, b, c):
        return ((a * 4 + b) * 2 + c, expert)

    to_x, to_up, to_dn, to_core = sec(ox, y, core), sec(xl, up, core), sec(xl, dn, core), sec(xl, y, 1 - core)

    barrier = pltpu.get_barrier_semaphore()
    for peer in (to_core, to_x, to_up, to_dn):
        pl.semaphore_signal(barrier, inc=1, device_id=peer, device_id_type=MESH)

    @pl.loop(1, 32)
    def _(place):
        pl.semaphore_signal(
            barrier, inc=1, device_id=(section, peer_expert(place, xh, z, 1)), device_id_type=MESH
        )

    loads = []
    for half, ref in enumerate((w_gate, w_up)):
        for c in range(2):
            loads.append(
                pltpu.make_async_copy(
                    ref.at[:, c],
                    wide.at[pl.ds(8 * c, 8), pl.ds(0, FEAT), pl.ds(128 * half, 128)],
                    w_sem.at[2 * half + c],
                )
            )
    loads.append(pltpu.make_async_copy(w_down, down_raw, w_sem.at[4]))
    for load in loads:
        load.start()

    def send(src, dst, send_sem, recv_sem, peer):
        pltpu.make_async_remote_copy(
            src_ref=src, dst_ref=dst, send_sem=send_sem, recv_sem=recv_sem, device_id=peer, device_id_type=MESH
        ).start()

    def await_bytes(ref, sem):
        pltpu.make_async_copy(ref, ref, sem).wait()

    keys_t = []
    named = [(iota((32, TOK), 0) == ids_t[k : k + 1, :]) for k in range(2)]
    before = dot(
        one_hot(named[0] | named[1]), one_hot(iota((TOK, TOK), 0) < iota((TOK, TOK), 1))
    )
    for k in range(2):
        number = jnp.sum(jnp.where(named[k], before, 0.0), axis=0, keepdims=True)
        keys_t.append(ids_t[k : k + 1, :] * 32 + number.astype(I32))
    row = iota((512, 1), 0)
    base, slot = peer_expert(row // 16, xh, z, -1) * 32, row % 16
    main_key = base + slot
    rest_key = jnp.where(slot < 14, base + 16 + (slot >= 7).astype(I32), -1)
    to_main = one_hot((keys_t[0] == main_key) | (keys_t[1] == main_key))
    to_rest = one_hot((keys_t[0] == rest_key) | (keys_t[1] == rest_key))
    widen = one_hot(iota((FEAT, LANES), 0) == iota((FEAT, LANES), 1))
    padded = dot(tokens[...], widen).astype(BF16)
    packed = dot(to_main, padded) + fold(dot(to_rest, padded))
    pack[...] = packed.astype(BF16).reshape(32, 16, LANES)
    arrived[0] = pack[0]

    pl.semaphore_wait(barrier, 35)

    @pl.loop(1, 32)
    def _(place):
        send(
            pack.at[place], arrived.at[place], z_send, z_recv.at[place // PER],
            (section, peer_expert(place, xh, z, -1)),
        )

    named = [(iota((TOK, 128), 1) == ids[:, k : k + 1]) for k in range(2)]
    before = dot(
        one_hot(iota((TOK, TOK), 1) < iota((TOK, TOK), 0)), one_hot(named[0] | named[1])
    )
    for k in range(2):
        number = jnp.sum(jnp.where(named[k], before, 0.0), axis=1, keepdims=True)
        key = ids[:, k : k + 1] * 32 + number.astype(I32)
        for q in range(GROUPS):
            column = iota((1, MAIN), 1) + q * MAIN
            base, slot = peer_expert(column // 16, xh, z, -1) * 32, column % 16
            rest_key = jnp.where(slot < 14, base + 16 + (slot >= 7).astype(I32), -1)
            picks[q, 0, pl.ds(k * TOK, TOK), :] = one_hot(key == base + slot)
            picks[q, 1, pl.ds(k * TOK, TOK), :] = one_hot(key == rest_key)
    total0[...] = jnp.zeros_like(total0)
    total1[...] = jnp.zeros_like(total1)

    gain_row = dot(jnp.broadcast_to(gain[...], (16, FEAT)), widen)[0:1, :]
    wide[:, FEAT:LANES, :] = jnp.zeros((16, LANES - FEAT, LANES), BF16)
    for load in loads:
        load.wait()
    for s in range(16):
        first = (s * FEAT) // 128 * 128
        shift = s * FEAT - first
        window = down_raw[:, first : first + (384 if shift else 256)] if first + 384 <= D or not shift else down_raw[:, first:D]
        piece = window.astype(F32)[:, shift : shift + FEAT]
        down[(s % 2) * 8 + s // 2, :, 0:FEAT] = piece.astype(BF16)
        down[(s % 2) * 8 + s // 2, :, FEAT:LANES] = jnp.zeros((128, LANES - FEAT), BF16)

    def chip(a, b):
        return a * 4 + b

    def block(q, a, b, c):
        return blocks.at[q, c * 8 + chip(a, b)]

    def share(q, a, b, peer, recv_sem):
        ref = block(q, a, b, core)
        send(ref, ref, g_send.at[q], recv_sem, peer)

    def to_peer(q, a, b):
        share(q, a, b, to_core, g_core.at[q])

    def unpack(q):
        @pl.when(q == 0)
        def _():
            await_bytes(arrived.at[pl.ds(1, PER - 1)], z_recv.at[0])

        @pl.when(q > 0)
        def _():
            await_bytes(arrived.at[pl.ds(q * PER, PER)], z_recv.at[q])

        got = arrived[pl.ds(q * PER, PER)].reshape(MAIN, LANES)
        lane = iota((ROWS, LANES), 1)
        row, col = iota((2 * PER, MAIN), 0), iota((2 * PER, MAIN), 1)
        slot = col % 16
        gather = one_hot((col // 16 == row // 2) & (slot < 14) & ((slot >= 7).astype(I32) == row % 2))
        rest = dot(gather, unfold(got))
        x = jnp.where(lane < FEAT, jnp.concatenate([got.astype(F32), rest], axis=0), 0.0)
        square = jnp.sum(x * x, axis=1, keepdims=True)
        high = square.astype(BF16).astype(F32)
        mid = (square - high).astype(BF16).astype(F32)
        low = square - high - mid
        x = x * gain_row
        x = jnp.where(lane == FEAT, high, x)
        x = jnp.where(lane == FEAT + 1, mid, x)
        x = jnp.where(lane == FEAT + 2, low, x)
        blocks[q, core * 8 + chip(xl, y)] = x.astype(BF16)
        share(q, xl, y, to_x, g_x.at[q])
        share(q, xl, y, to_up, g_y.at[q, 0])
        share(q, xl, y, to_dn, g_y.at[q, 2])
        to_peer(q, xl, y)

    def gather_x(q):
        await_bytes(block(q, ox, y, core), g_x.at[q])
        share(q, ox, y, to_up, g_y.at[q, 3])
        share(q, ox, y, to_dn, g_y.at[q, 1])
        to_peer(q, ox, y)

    def gather_y(q):
        await_bytes(block(q, xl, dn, core), g_y.at[q, 0])
        share(q, xl, dn, to_up, g_y.at[q, 4])
        await_bytes(block(q, ox, up, core), g_y.at[q, 1])
        share(q, ox, up, to_dn, g_y.at[q, 5])
        to_peer(q, xl, dn)
        to_peer(q, ox, up)
        await_bytes(block(q, xl, up, core), g_y.at[q, 2])
        to_peer(q, xl, up)
        await_bytes(block(q, ox, dn, core), g_y.at[q, 3])
        to_peer(q, ox, dn)

    def gather_far(q):
        await_bytes(block(q, xl, far, core), g_y.at[q, 4])
        to_peer(q, xl, far)
        await_bytes(block(q, ox, far, core), g_y.at[q, 5])
        to_peer(q, ox, far)

    def compute(q):
        await_bytes(blocks.at[q, pl.ds((1 - core) * 8, 8)], g_core.at[q])
        product = jnp.zeros((ROWS, LANES), F32)
        squares = jnp.zeros((ROWS, 128), F32)
        for k in range(16):
            x = blocks[q, k]
            product = product + dot(x, wide[k])
            squares = squares + x[:, 128:256].astype(F32)
        lane = iota((ROWS, 128), 1)
        kept = (lane >= FEAT - 128) & (lane < FEAT - 128 + 3)
        square = jnp.sum(jnp.where(kept, squares, 0.0), axis=1, keepdims=True)
        scale = lax.rsqrt(square * (1.0 / D) + epsilon)
        gate, upward = product[:, 0:128] * scale, product[:, 128:256] * scale
        hidden[...] = (gate / (1.0 + jnp.exp(-gate)) * upward).astype(BF16)
        for k in range(8):
            core_out[q, k] = dot(hidden[...], down[(1 - core) * 8 + k]).astype(BF16)
        send(core_out.at[q], core_in.at[q], p_send.at[q], p_recv.at[q], to_core)

    def add_core(q):
        await_bytes(core_in.at[q], p_recv.at[q])
        for k in range(8):
            own = dot(hidden[...], down[core * 8 + k])
            sums[q, k] = (own + core_in[q, k].astype(F32)).astype(BF16)
        send(sums.at[q, chip(xl, far)], y_in.at[q, 0], r_send.at[q], r_recv.at[q, 0], to_up)
        send(sums.at[q, chip(ox, far)], y_in.at[q, 1], r_send.at[q], r_recv.at[q, 1], to_dn)
        send(sums.at[q, chip(ox, up)], y_in.at[q, 2], r_send.at[q], r_recv.at[q, 2], to_up)
        send(sums.at[q, chip(xl, dn)], y_in.at[q, 3], r_send.at[q], r_recv.at[q, 3], to_dn)

    def add_far(q):
        for j, where_to, peer in ((0, chip(xl, up), to_up), (1, chip(ox, dn), to_dn)):
            await_bytes(y_in.at[q, j], r_recv.at[q, j])
            sums[q, where_to] = (sums[q, where_to].astype(F32) + y_in[q, j].astype(F32)).astype(BF16)
            send(sums.at[q, where_to], y_in.at[q, 4 + j], r_send.at[q], r_recv.at[q, 4 + j], peer)

    def add_y(q):
        for j in (2, 5):
            await_bytes(y_in.at[q, j], r_recv.at[q, j])
        x_out[q] = (
            sums[q, chip(ox, y)].astype(F32) + y_in[q, 2].astype(F32) + y_in[q, 5].astype(F32)
        ).astype(BF16)
        send(x_out.at[q], x_in.at[q], x_send.at[q], x_recv.at[q], to_x)
        for j in (3, 4):
            await_bytes(y_in.at[q, j], r_recv.at[q, j])

    def add_x(q):
        own = sums[q, chip(xl, y)].astype(F32) + y_in[q, 3].astype(F32) + y_in[q, 4].astype(F32)
        await_bytes(x_in.at[q], x_recv.at[q])
        total = own + x_in[q].astype(F32)
        row, col = iota((MAIN, 2 * PER), 0), iota((MAIN, 2 * PER), 1)
        slot = row % 16
        spread = one_hot((row // 16 == col // 2) & (slot < 14) & ((slot >= 7).astype(I32) == col % 2))
        packed = total[0:MAIN] + fold(dot(spread, total[MAIN:ROWS].astype(BF16)))
        back[pl.ds(q * PER, PER)] = packed.astype(BF16).reshape(PER, 16, LANES)

        @pl.when(q == 0)
        def _():
            returned[0] = back[0]

        @pl.loop(jnp.where(q == 0, 1, 0), PER)
        def _(k):
            place = q * PER + k
            send(
                back.at[place], returned.at[place], b_send, b_recv.at[q],
                (section, peer_expert(place, xh, z, 1)),
            )

    def mix(q):
        @pl.when(q == 0)
        def _():
            await_bytes(returned.at[pl.ds(1, PER - 1)], b_recv.at[0])

        @pl.when(q > 0)
        def _():
            await_bytes(returned.at[pl.ds(q * PER, PER)], b_recv.at[q])

        got = returned[pl.ds(q * PER, PER)].reshape(MAIN, LANES)
        picked = dot(picks[q, 0], got) + dot(picks[q, 1], unfold(got))
        total0[...] += picked[0:TOK]
        total1[...] += picked[TOK : 2 * TOK]

    stages = (unpack, gather_x, gather_y, gather_far, compute, add_core, add_far, add_y, add_x, mix)
    skew = (0, 1, 2, 3, 3, 4, 5, 6, 7, 8)

    @pl.loop(0, GROUPS + skew[-1])
    def _(step):
        for stage, late in sorted(zip(stages, skew), key=lambda pair: -pair[1]):
            q = step - late

            @pl.when((q >= 0) & (q < GROUPS))
            def _():
                stage(q)

    mixed = gate_weight[:, 0:1] * total0[...] + gate_weight[:, 1:2] * total1[...]
    out[...] = mixed[:, 0:FEAT].astype(BF16)

    await_bytes(pack.at[pl.ds(1, 31)], z_send)
    await_bytes(back.at[pl.ds(1, 31)], b_send)

    @pl.loop(0, GROUPS)
    def _(q):
        await_bytes(blocks.at[q, pl.ds(0, 15)], g_send.at[q])
        await_bytes(core_out.at[q], p_send.at[q])
        await_bytes(y_in.at[q], r_send.at[q])
        await_bytes(x_out.at[q], x_send.at[q])


def on_device(tokens, norm_gain, expert_ids, gate_weight, w_gate, w_up, w_down):
    vmem = pl.BlockSpec(memory_space=pltpu.VMEM)
    anywhere = pl.BlockSpec(memory_space=pl.ANY)
    dma = pltpu.SemaphoreType.DMA
    block = (ROWS, LANES)
    return pl.pallas_call(
        kernel,
        out_shape=jax.ShapeDtypeStruct((TOK, FEAT), BF16),
        in_specs=[vmem] * 5 + [anywhere] * 3,
        out_specs=vmem,
        scratch_shapes=[
            pltpu.VMEM((32, 16, LANES), BF16),
            pltpu.VMEM((32, 16, LANES), BF16),
            pltpu.VMEM((GROUPS, 16) + block, BF16),
            pltpu.VMEM((16, LANES, LANES), BF16),
            pltpu.VMEM((16, 128, LANES), BF16),
            pltpu.VMEM((128, D), BF16),
            pltpu.VMEM((ROWS, 128), BF16),
            pltpu.VMEM((GROUPS, 8) + block, BF16),
            pltpu.VMEM((GROUPS, 8) + block, BF16),
            pltpu.VMEM((GROUPS, 8) + block, BF16),
            pltpu.VMEM((GROUPS, 6) + block, BF16),
            pltpu.VMEM((GROUPS,) + block, BF16),
            pltpu.VMEM((GROUPS,) + block, BF16),
            pltpu.VMEM((32, 16, LANES), BF16),
            pltpu.VMEM((32, 16, LANES), BF16),
            pltpu.VMEM((GROUPS, 2, 2 * TOK, MAIN), BF16),
            pltpu.VMEM((TOK, LANES), F32),
            pltpu.VMEM((TOK, LANES), F32),
            dma((5,)), dma, dma((GROUPS,)),
            dma((GROUPS,)), dma((GROUPS,)), dma((GROUPS, 6)), dma((GROUPS,)),
            dma((GROUPS,)), dma((GROUPS,)),
            dma((GROUPS,)), dma((GROUPS, 6)),
            dma((GROUPS,)), dma((GROUPS,)),
            dma, dma((GROUPS,)),
        ],
        compiler_params=pltpu.CompilerParams(
            collective_id=0, has_side_effects=True, vmem_limit_bytes=48 * 1024 * 1024
        ),
        cost_estimate=pl.CostEstimate(flops=2_000_000_000, bytes_accessed=3_000_000, transcendentals=73728),
    )(
        tokens, expert_ids, expert_ids.T, gate_weight, norm_gain,
        w_gate.reshape(8, 2, FEAT, 128), w_up.reshape(8, 2, FEAT, 128), w_down[0],
    )


def solution(mesh):
    placed = (
        P("expert", "section"),
        P(None, "section"),
        P("expert", None),
        P("expert", None),
        P("expert", None, "section"),
        P("expert", None, "section"),
        P("expert", "section", None),
    )
    return jax.shard_map(
        on_device, mesh=mesh, in_specs=placed, out_specs=P("expert", "section"), check_vma=False
    )
```

time: 245 us -> 103 us (0.42)
  the two profiles are of different devices: /device:TPU:6 before, /device:TPU:32 now
where the time goes in v2:
time: 103 us; the launch traced here: 102 us
  Pallas kernels  96 us (93%)
  local copies, waits for them, and re-layouts  6.2 us (6%)
    pallas_call x1, Pallas kernels, on_device(): pl.pallas_call(kernel, out_shape=jax.ShapeDtypeStruct((TOK, FEAT), BF16),...  96 us
    unnamed x17, local copies, waits for them, and re-layouts  6.2 us

profile of v2, /device:TPU:32, one launch (start us, length us, event | category | flops | bytes accessed | tf_op | source)
XLA Modules:
  0.0 102.2 jit_solution(13443840128560943564)
XLA Ops:
  0.0 0.0 copy-start.6
  0.0 0.7 copy-done.6
  0.7 0.0 copy-start
  0.7 0.0 copy-start.4
  0.7 0.1 copy.9.gate_weight
  0.8 0.6 copy-done
  1.4 0.0 copy-start.5
  1.4 0.1 copy.8.ids
  1.5 0.1 copy-done.4
  1.6 0.5 copy-done.5
  2.1 0.0 copy-start.1
  2.1 1.2 %copy-done.1 = bf16[1,3584,128]{2,1,0:T(8,128)(2,1)S(1)} copy-done((bf16[1,3584,128]{2,1,0:T(8,128)(2,1)S(1)}, bf16[1,3584,128]{2,1,0:T(8,128)(2,1)}, u32[]{:S(2)}) %copy-start.1) | copy-done | bytes 917528
  3.2 0.0 copy-start.2
  3.2 1.2 %copy-done.2 = bf16[1,3584,128]{2,1,0:T(8,128)(2,1)S(1)} copy-done((bf16[1,3584,128]{2,1,0:T(8,128)(2,1)S(1)}, bf16[1,3584,128]{2,1,0:T(8,128)(2,1)}, u32[]{:S(2)}) %copy-start.2) | copy-done | bytes 917528
  4.4 0.0 copy-start.3
  4.4 1.2 %copy-done.3 = bf16[1,128,3584]{2,1,0:T(8,128)(2,1)S(1)} copy-done((bf16[1,128,3584]{2,1,0:T(8,128)(2,1)S(1)}, bf16[1,128,3584]{2,1,0:T(8,128)(2,1)}, u32[]{:S(2)}) %copy-start.3) | copy-done | bytes 917528
  5.6 96.0 %shard_map.73 = bf16[144,224]{1,0:T(8,128)(2,1)S(1)} custom-call(bf16[144,224]{1,0:T(8,128)(2,1)S(1)} %copy-done.4, s32[144,2]{1,0:T(8,128)S(1)} %copy.8.ids, s32[2,144]{1,0:T(2,128)S(1)} %bitcast.4, f32[144,2]{1,0:T(8,128)S(1)} %copy.9.gate_weight, bf16[1,224]{1,0:T(2,128)(2,1)S(1)} %copy-done.5, bf16[8,2,224,128]{3,2,1,0:T(8,128)(2,1)S(1)} %bitcast.5, ...), custom_call_target="tpu_custom_call" | custom-call | flops 2000000000 | bytes 3000000 | tf_op jit(solution)/shard_map/pallas_call | solution.py:352
  101.6 0.6 copy.11
Async XLA Ops:
  0.0 0.7 copy-start.6
  0.7 0.7 copy-start
  0.7 0.9 copy-start.4
  1.4 0.7 copy-start.5
  2.1 1.2 %copy-start.1 = (bf16[1,3584,128]{2,1,0:T(8,128)(2,1)S(1)}, bf16[1,3584,128]{2,1,0:T(8,128)(2,1)}, u32[]{:S(2)}) copy-start(bf16[1,3584,128]{2,1,0:T(8,128)(2,1)} %param.11) | copy-start | bytes 2752516
  3.2 1.2 %copy-start.2 = (bf16[1,3584,128]{2,1,0:T(8,128)(2,1)S(1)}, bf16[1,3584,128]{2,1,0:T(8,128)(2,1)}, u32[]{:S(2)}) copy-start(bf16[1,3584,128]{2,1,0:T(8,128)(2,1)} %param.12) | copy-start | bytes 2752516
  4.4 1.2 %copy-start.3 = (bf16[1,128,3584]{2,1,0:T(8,128)(2,1)S(1)}, bf16[1,128,3584]{2,1,0:T(8,128)(2,1)}, u32[]{:S(2)}) copy-start(bf16[1,128,3584]{2,1,0:T(8,128)(2,1)} %param.13) | copy-start | bytes 2752516

commit v3 on v2

v3 whole, which is shorter than its diff:
```python
import jax
import jax.numpy as jnp
from jax import lax
from jax.experimental import pallas as pl
from jax.experimental.pallas import tpu as pltpu
from jax.sharding import PartitionSpec as P

epsilon = 1e-06
D = 3584
FEAT = 224
LANES = 256
TOK = 144
SLOTS = 16
GROUPS = 4
PER = 8
MAIN = PER * SLOTS
ROWS = MAIN + 2 * PER
F32 = jnp.float32
BF16 = jnp.bfloat16
I32 = jnp.int32
MESH = pl.DeviceIdType.MESH
SEND_ORDER = (0, 3, 2, 1)
GATHER_X_FIRST = (True, True, False, True)
SCATTER_X_FIRST = (False, False, False, True)
ORDER = (
    ("U", 0), ("W", 0), ("X", 0), ("Y0", 0), ("Y2", 0), ("U", 3), ("K", 0), ("Y3", 0), ("Y1", 0), ("F0", 0),
    ("X", 3), ("Y2", 3), ("U", 2), ("Y0", 3), ("F1", 0), ("U", 1), ("C", 0), ("Y1", 3), ("Y3", 3), ("y0", 2),
    ("x0", 2), ("X", 1), ("F0", 3), ("Y2", 1), ("R1", 0), ("Y0", 1), ("x1", 2), ("F1", 3), ("f0", 2), ("C", 3),
    ("Y1", 1), ("Y3", 1), ("x2", 2), ("R2a", 0), ("x3", 2), ("R2b", 0), ("R1", 3), ("C", 2), ("F0", 1), ("F1", 1),
    ("r2", 3), ("R3", 0), ("R1", 2), ("C", 1), ("r3", 3), ("R2a", 2), ("R2b", 2), ("R1", 1), ("R4", 0), ("R4", 3),
    ("Z", 0), ("R3", 2), ("R2a", 1), ("R2b", 1), ("R4", 2), ("R3", 1), ("Z", 3), ("R4", 1), ("Z", 2), ("Z", 1),
)


def iota(shape, dim):
    return lax.broadcasted_iota(I32, shape, dim)


def one_hot(mask):
    return jnp.where(mask, 1.0, 0.0).astype(BF16)


def dot(a, b):
    return jnp.dot(a, b, preferred_element_type=F32)


def peer_expert(place, xh, z, sign):
    step = place // 2
    half = (step + 1) // 2
    offset = half * (2 * (step % 2) - 1)
    return ((xh + place % 2) % 2) * 16 + (z + sign * offset + 16) % 16


def piece_of(slot):
    return slot - 7 * (slot >= 7).astype(I32)


def unfold(packed):
    rows = packed.shape[0]
    lane = iota((128, LANES), 1)
    spread = one_hot((iota((128, LANES), 0) - 96 == lane % 32) & (lane < FEAT))
    copies = dot(packed[:, 128:256], spread)
    slot = iota((rows, LANES), 0) % 16
    keep = (iota((rows, LANES), 1) // 32 == piece_of(slot)) & (slot < 14)
    return jnp.where(keep, copies, 0.0).astype(BF16)


def fold(spread):
    rows, width = spread.shape
    slot = iota((rows, width), 0) % 16
    keep = (iota((rows, width), 1) // 32 == piece_of(slot)) & (slot < 14)
    own = jnp.where(keep, spread, 0.0).astype(BF16)
    lane = iota((width, LANES), 1)
    gather = one_hot((lane >= FEAT) & (iota((width, LANES), 0) % 32 == lane - FEAT))
    return dot(own, gather)


def kernel(
    tokens_hbm, ids_hbm, gate_hbm, gain_hbm, w_gate, w_up, w_down, out,
    tokens, ids, gate_weight, gain,
    pack, arrived, blocks, wide, down, down_raw, hidden, core_out, core_in, sums, partial_in, x_out,
    back, returned, picks, total0, total1,
    in_sem, w_sem, z_send, z_recv, g_send, g_x, g_y, g_core, p_send, p_recv, r_send, r_recv,
    b_send, b_recv,
):
    section, expert = lax.axis_index("section"), lax.axis_index("expert")
    xl, y, core = section // 8, (section // 2) % 4, section % 2
    xh, z = expert // 16, expert % 16
    up, dn, far = (y + 1) % 4, (y + 3) % 4, (y + 2) % 4
    ox = 1 - xl
    onward, behind = jnp.where(core == 0, up, dn), jnp.where(core == 0, dn, up)

    def sec(a, b, c):
        return ((a * 4 + b) * 2 + c, expert)

    to_x, to_up, to_dn, to_core = sec(ox, y, core), sec(xl, up, core), sec(xl, dn, core), sec(xl, y, 1 - core)
    to_onward = sec(xl, onward, core)

    inputs = []
    for j, (src, dst) in enumerate(((ids_hbm, ids), (tokens_hbm, tokens), (gain_hbm, gain), (gate_hbm, gate_weight))):
        inputs.append(pltpu.make_async_copy(src, dst, in_sem.at[j]))
    loads = []
    for half, ref in enumerate((w_gate, w_up)):
        for c in range(2):
            loads.append(
                pltpu.make_async_copy(
                    ref.at[:, c],
                    wide.at[pl.ds(8 * c, 8), pl.ds(0, FEAT), pl.ds(128 * half, 128)],
                    w_sem.at[2 * half + c],
                )
            )
    loads.append(pltpu.make_async_copy(w_down, down_raw, w_sem.at[4]))
    for load in inputs + loads:
        load.start()

    barrier = pltpu.get_barrier_semaphore()
    for peer in (to_core, to_x, to_up, to_dn):
        pl.semaphore_signal(barrier, inc=1, device_id=peer, device_id_type=MESH)

    @pl.loop(1, 32)
    def _(place):
        pl.semaphore_signal(
            barrier, inc=1, device_id=(section, peer_expert(place, xh, z, 1)), device_id_type=MESH
        )

    def send(src, dst, send_sem, recv_sem, peer):
        pltpu.make_async_remote_copy(
            src_ref=src, dst_ref=dst, send_sem=send_sem, recv_sem=recv_sem, device_id=peer, device_id_type=MESH
        ).start()

    def await_bytes(ref, sem):
        pltpu.make_async_copy(ref, ref, sem).wait()

    for load in inputs:
        load.wait()
    keys = []
    named = [(iota((32, TOK), 0) == ids[k : k + 1, :]) for k in range(2)]
    before = dot(
        one_hot(named[0] | named[1]), one_hot(iota((TOK, TOK), 0) < iota((TOK, TOK), 1))
    )
    for k in range(2):
        number = jnp.sum(jnp.where(named[k], before, 0.0), axis=0, keepdims=True)
        keys.append(ids[k : k + 1, :] * 32 + number.astype(I32))
    row = iota((512, 1), 0)
    base, slot = peer_expert(row // 16, xh, z, -1) * 32, row % 16
    main_key = base + slot
    rest_key = jnp.where(slot < 14, base + 16 + (slot >= 7).astype(I32), -1)
    to_main = one_hot((keys[0] == main_key) | (keys[1] == main_key))
    to_rest = one_hot((keys[0] == rest_key) | (keys[1] == rest_key))
    widen = one_hot(iota((FEAT, LANES), 0) == iota((FEAT, LANES), 1))
    padded = dot(tokens[...], widen).astype(BF16)
    packed = dot(to_main, padded) + fold(dot(to_rest, padded))
    pack[...] = packed.astype(BF16).reshape(32, 16, LANES)
    arrived[0] = pack[0]
    gain_row = dot(jnp.broadcast_to(gain[...], (16, FEAT)), widen)[0:1, :]

    pl.semaphore_wait(barrier, 35)

    for q in SEND_ORDER:

        @pl.loop(q * PER + (1 if q == 0 else 0), q * PER + PER)
        def _(place):
            send(
                pack.at[place], arrived.at[place], z_send, z_recv.at[q],
                (section, peer_expert(place, xh, z, -1)),
            )

    def column_of(line):
        same = iota((TOK, TOK), 0) == iota((TOK, TOK), 1)
        return jnp.sum(jnp.where(same, line, jnp.zeros_like(line)), axis=1, keepdims=True)

    def prepare_mix(_):
        for k in range(2):
            key = column_of(keys[k].astype(F32)).astype(I32)
            for q in range(GROUPS):
                column = iota((1, MAIN), 1) + q * MAIN
                base, slot = peer_expert(column // 16, xh, z, -1) * 32, column % 16
                rest_key = jnp.where(slot < 14, base + 16 + (slot >= 7).astype(I32), -1)
                picks[q, 0, pl.ds(k * TOK, TOK), :] = one_hot(key == base + slot)
                picks[q, 1, pl.ds(k * TOK, TOK), :] = one_hot(key == rest_key)
        total0[...] = jnp.zeros_like(total0)
        total1[...] = jnp.zeros_like(total1)

    def prepare_weights(_):
        wide[:, FEAT:LANES, :] = jnp.zeros((16, LANES - FEAT, LANES), BF16)
        for load in loads:
            load.wait()
        for s in range(16):
            first = (s * FEAT) // 128 * 128
            shift = s * FEAT - first
            window = down_raw[:, first : min(first + 384, D)]
            place = (s % 2) * 8 + s // 2
            down[place, :, 0:FEAT] = window.astype(F32)[:, shift : shift + FEAT].astype(BF16)
            down[place, :, FEAT:LANES] = jnp.zeros((128, LANES - FEAT), BF16)

    def chip(a, b):
        return a * 4 + b

    def block(q, a, b, c):
        return blocks.at[q, c * 8 + chip(a, b)]

    def share(q, a, b, peer, recv_sem):
        ref = block(q, a, b, core)
        send(ref, ref, g_send.at[q], recv_sem, peer)

    def to_peer(q, a, b):
        share(q, a, b, to_core, g_core.at[q])

    def unpack(q):
        skip = 1 if q == 0 else 0
        await_bytes(arrived.at[pl.ds(q * PER + skip, PER - skip)], z_recv.at[q])
        got = arrived[pl.ds(q * PER, PER)].reshape(MAIN, LANES)
        lane = iota((ROWS, LANES), 1)
        row, col = iota((2 * PER, MAIN), 0), iota((2 * PER, MAIN), 1)
        slot = col % 16
        gather = one_hot((col // 16 == row // 2) & (slot < 14) & ((slot >= 7).astype(I32) == row % 2))
        rest = dot(gather, unfold(got))
        x = jnp.where(lane < FEAT, jnp.concatenate([got.astype(F32), rest], axis=0), 0.0)
        square = jnp.sum(x * x, axis=1, keepdims=True)
        high = square.astype(BF16).astype(F32)
        mid = (square - high).astype(BF16).astype(F32)
        low = square - high - mid
        x = x * gain_row
        x = jnp.where(lane == FEAT, high, x)
        x = jnp.where(lane == FEAT + 1, mid, x)
        x = jnp.where(lane == FEAT + 2, low, x)
        blocks[q, core * 8 + chip(xl, y)] = x.astype(BF16)
        share(q, xl, y, to_x, g_x.at[q, 0])
        share(q, xl, y, to_up, g_y.at[q, 0])
        share(q, xl, y, to_dn, g_y.at[q, 1])
        to_peer(q, xl, y)

    def x_then_y(q):
        await_bytes(block(q, ox, y, core), g_x.at[q, 0])
        share(q, ox, y, to_up, g_y.at[q, 2])
        share(q, ox, y, to_dn, g_y.at[q, 3])
        to_peer(q, ox, y)

    def relay_up(q):
        await_bytes(block(q, xl, dn, core), g_y.at[q, 0])
        share(q, xl, dn, to_up, g_y.at[q, 4])
        to_peer(q, xl, dn)

    def relay_dn(q):
        await_bytes(block(q, ox, up, core), g_y.at[q, 3])
        share(q, ox, up, to_dn, g_y.at[q, 5])
        to_peer(q, ox, up)

    def keep(q, a, b, sem):
        await_bytes(block(q, a, b, core), sem)
        to_peer(q, a, b)

    def y_then_x(q):
        await_bytes(block(q, xl, dn, core), g_y.at[q, 0])
        await_bytes(block(q, xl, up, core), g_y.at[q, 1])
        share(q, xl, behind, to_onward, g_y.at[q, 2])
        share(q, xl, dn, to_x, g_x.at[q, 1])
        share(q, xl, up, to_x, g_x.at[q, 2])
        to_peer(q, xl, dn)
        to_peer(q, xl, up)

    def far_then_x(q):
        await_bytes(block(q, xl, far, core), g_y.at[q, 2])
        share(q, xl, far, to_x, g_x.at[q, 3])
        to_peer(q, xl, far)

    def compute(q):
        await_bytes(blocks.at[q, pl.ds((1 - core) * 8, 8)], g_core.at[q])
        product = jnp.zeros((ROWS, LANES), F32)
        squares = jnp.zeros((ROWS, 128), F32)
        for k in range(16):
            x = blocks[q, k]
            product = product + dot(x, wide[k])
            squares = squares + x[:, 128:256].astype(F32)
        lane = iota((ROWS, 128), 1)
        kept = (lane >= FEAT - 128) & (lane < FEAT - 128 + 3)
        square = jnp.sum(jnp.where(kept, squares, 0.0), axis=1, keepdims=True)
        scale = lax.rsqrt(square * (1.0 / D) + epsilon)
        gate, upward = product[:, 0:128] * scale, product[:, 128:256] * scale
        hidden[q] = (gate / (1.0 + jnp.exp(-gate)) * upward).astype(BF16)
        for k in range(8):
            core_out[q, k] = dot(hidden[q], down[(1 - core) * 8 + k]).astype(BF16)
        send(core_out.at[q], core_in.at[q], p_send.at[q], p_recv.at[q], to_core)

    def pass_on(q, place, j, peer):
        send(sums.at[q, place], partial_in.at[q, j], r_send.at[q], r_recv.at[q, j], peer)

    def take(q, j):
        await_bytes(partial_in.at[q, j], r_recv.at[q, j])
        return partial_in[q, j].astype(F32)

    def add_core(q):
        await_bytes(core_in.at[q], p_recv.at[q])
        for k in range(8):
            own = dot(hidden[q], down[core * 8 + k])
            sums[q, k] = (own + core_in[q, k].astype(F32)).astype(BF16)
        if SCATTER_X_FIRST[q]:
            for j, b in enumerate((far, up, dn, y)):
                pass_on(q, chip(ox, b), j, to_x)
        else:
            pass_on(q, chip(xl, far), 0, to_up)
            pass_on(q, chip(ox, far), 1, to_dn)
            pass_on(q, chip(ox, up), 2, to_up)
            pass_on(q, chip(xl, dn), 3, to_dn)

    def add_into(q, place, j):
        sums[q, place] = (sums[q, place].astype(F32) + take(q, j)).astype(BF16)

    def far_up(q):
        add_into(q, chip(xl, up), 0)
        pass_on(q, chip(xl, up), 4, to_up)

    def far_dn(q):
        add_into(q, chip(ox, dn), 1)
        pass_on(q, chip(ox, dn), 5, to_dn)

    def y_sum(q):
        x_out[q] = (sums[q, chip(ox, y)].astype(F32) + take(q, 2) + take(q, 5)).astype(BF16)
        send(x_out.at[q], partial_in.at[q, 6], r_send.at[q], r_recv.at[q, 6], to_x)

    def x_far(q):
        add_into(q, chip(xl, far), 0)
        pass_on(q, chip(xl, far), 4, to_onward)

    def x_near(q):
        add_into(q, chip(xl, up), 1)
        add_into(q, chip(xl, dn), 2)
        add_into(q, chip(xl, onward), 4)
        pass_on(q, chip(xl, up), 5, to_up)
        pass_on(q, chip(xl, dn), 6, to_dn)

    def finish(q):
        total = sums[q, chip(xl, y)].astype(F32)
        for j in (3, 5, 6) if SCATTER_X_FIRST[q] else (3, 4, 6):
            total = total + take(q, j)
        row, col = iota((MAIN, 2 * PER), 0), iota((MAIN, 2 * PER), 1)
        slot = row % 16
        spread = one_hot((row // 16 == col // 2) & (slot < 14) & ((slot >= 7).astype(I32) == col % 2))
        packed = total[0:MAIN] + fold(dot(spread, total[MAIN:ROWS].astype(BF16)))
        back[pl.ds(q * PER, PER)] = packed.astype(BF16).reshape(PER, 16, LANES)
        if q == 0:
            returned[0] = back[0]

        @pl.loop(q * PER + (1 if q == 0 else 0), q * PER + PER)
        def _(place):
            send(
                back.at[place], returned.at[place], b_send, b_recv.at[q],
                (section, peer_expert(place, xh, z, 1)),
            )

    def mix(q):
        skip = 1 if q == 0 else 0
        await_bytes(returned.at[pl.ds(q * PER + skip, PER - skip)], b_recv.at[q])
        got = returned[pl.ds(q * PER, PER)].reshape(MAIN, LANES)
        picked = dot(picks[q, 0], got) + dot(picks[q, 1], unfold(got))
        total0[...] += picked[0:TOK]
        total1[...] += picked[TOK : 2 * TOK]

    tasks = {
        "W": prepare_weights, "K": prepare_mix,
        "U": unpack, "C": compute, "R1": add_core, "R4": finish, "Z": mix,
        "X": x_then_y, "Y0": relay_up, "Y1": relay_dn,
        "Y2": lambda q: keep(q, xl, up, g_y.at[q, 1]), "Y3": lambda q: keep(q, ox, dn, g_y.at[q, 2]),
        "F0": lambda q: keep(q, xl, far, g_y.at[q, 4]), "F1": lambda q: keep(q, ox, far, g_y.at[q, 5]),
        "y0": y_then_x, "f0": far_then_x,
        "x0": lambda q: keep(q, ox, y, g_x.at[q, 0]),
        "x1": lambda q: keep(q, ox, dn, g_x.at[q, 1]),
        "x2": lambda q: keep(q, ox, up, g_x.at[q, 2]),
        "x3": lambda q: keep(q, ox, far, g_x.at[q, 3]),
        "R2a": far_up, "R2b": far_dn, "R3": y_sum, "r2": x_far, "r3": x_near,
    }
    for name, q in ORDER:
        tasks[name](q)

    weights = [column_of(gate_weight[k : k + 1, :]) for k in range(2)]
    mixed = weights[0] * total0[...] + weights[1] * total1[...]
    out[...] = mixed[:, 0:FEAT].astype(BF16)

    await_bytes(pack.at[pl.ds(1, 31)], z_send)
    await_bytes(back.at[pl.ds(1, 31)], b_send)
    for q in range(GROUPS):
        await_bytes(blocks.at[q, pl.ds(0, 15)], g_send.at[q])
        await_bytes(core_out.at[q], p_send.at[q])
        await_bytes(partial_in.at[q], r_send.at[q])


def on_device(tokens, norm_gain, expert_ids, gate_weight, w_gate, w_up, w_down):
    dma = pltpu.SemaphoreType.DMA
    block = (ROWS, LANES)
    return pl.pallas_call(
        kernel,
        out_shape=jax.ShapeDtypeStruct((TOK, FEAT), BF16),
        in_specs=[pl.BlockSpec(memory_space=pl.ANY)] * 7,
        out_specs=pl.BlockSpec(memory_space=pltpu.VMEM),
        scratch_shapes=[
            pltpu.VMEM((TOK, FEAT), BF16),
            pltpu.VMEM((2, TOK), I32),
            pltpu.VMEM((2, TOK), F32),
            pltpu.VMEM((1, FEAT), BF16),
            pltpu.VMEM((32, 16, LANES), BF16),
            pltpu.VMEM((32, 16, LANES), BF16),
            pltpu.VMEM((GROUPS, 16) + block, BF16),
            pltpu.VMEM((16, LANES, LANES), BF16),
            pltpu.VMEM((16, 128, LANES), BF16),
            pltpu.VMEM((128, D), BF16),
            pltpu.VMEM((GROUPS, ROWS, 128), BF16),
            pltpu.VMEM((GROUPS, 8) + block, BF16),
            pltpu.VMEM((GROUPS, 8) + block, BF16),
            pltpu.VMEM((GROUPS, 8) + block, BF16),
            pltpu.VMEM((GROUPS, 7) + block, BF16),
            pltpu.VMEM((GROUPS,) + block, BF16),
            pltpu.VMEM((32, 16, LANES), BF16),
            pltpu.VMEM((32, 16, LANES), BF16),
            pltpu.VMEM((GROUPS, 2, 2 * TOK, MAIN), BF16),
            pltpu.VMEM((TOK, LANES), F32),
            pltpu.VMEM((TOK, LANES), F32),
            dma((4,)), dma((5,)), dma, dma((GROUPS,)),
            dma((GROUPS,)), dma((GROUPS, 4)), dma((GROUPS, 6)), dma((GROUPS,)),
            dma((GROUPS,)), dma((GROUPS,)),
            dma((GROUPS,)), dma((GROUPS, 7)),
            dma, dma((GROUPS,)),
        ],
        compiler_params=pltpu.CompilerParams(
            collective_id=0, has_side_effects=True, vmem_limit_bytes=60 * 1024 * 1024
        ),
        cost_estimate=pl.CostEstimate(flops=2_000_000_000, bytes_accessed=3_000_000, transcendentals=73728),
    )(
        tokens, expert_ids.T, gate_weight.T, norm_gain,
        w_gate.reshape(8, 2, FEAT, 128), w_up.reshape(8, 2, FEAT, 128), w_down[0],
    )


def solution(mesh):
    placed = (
        P("expert", "section"),
        P(None, "section"),
        P("expert", None),
        P("expert", None),
        P("expert", None, "section"),
        P("expert", None, "section"),
        P("expert", "section", None),
    )
    return jax.shard_map(
        on_device, mesh=mesh, in_specs=placed, out_specs=P("expert", "section"), check_vma=False
    )
```

time: 103 us -> 85.3 us (0.83)
  the two profiles are of different devices: /device:TPU:32 before, /device:TPU:6 now
where the time goes in v3:
time: 85.3 us; the launch traced here: 84.8 us
  Pallas kernels  83.3 us (98%)
  local copies, waits for them, and re-layouts  1.52 us (2%)
    pallas_call x1, Pallas kernels, on_device(): pl.pallas_call(kernel, out_shape=jax.ShapeDtypeStruct((TOK, FEAT), BF16),...  83.3 us

profile of v3, /device:TPU:6, one launch (start us, length us, event | category | flops | bytes accessed | tf_op | source)
XLA Modules:
  0.0 84.8 jit_solution(8179540990169993764)
XLA Ops:
  0.0 83.3 %shard_map.73 = bf16[144,224]{1,0:T(8,128)(2,1)} custom-call(bf16[144,224]{1,0:T(8,128)(2,1)} %tokens_hbm.1, s32[2,144]{1,0:T(2,128)} %bitcast.8, f32[2,144]{1,0:T(2,128)} %bitcast.9, bf16[1,224]{1,0:T(2,128)(2,1)} %gain_hbm.1, bf16[8,2,224,128]{3,2,1,0:T(8,128)(2,1)} %bitcast.5, bf16[8,2,224,128]{3,2,1,0:T(8,128)(2,1)} %bitcast.6, bf16[128,3584]{1,0:T(8,128)(2,1)} %bitcast.7), custom_call_target="tpu_custom_call" | custom-call | flops 2000000000 | bytes 3000000 | tf_op jit(solution)/shard_map/pallas_call | solution.py:390
  83.3 1.5 %copy.9 = bf16[144,224]{1,0:T(8,128)(2,1)} copy(bf16[144,224]{1,0:T(8,128)(2,1)} %shard_map.73) | data formatting | bytes 129024

commit v4 on v3

--- a/solution.py
+++ b/solution.py
@@ -20,15 +20,12 @@
 I32 = jnp.int32
 MESH = pl.DeviceIdType.MESH
 SEND_ORDER = (0, 3, 2, 1)
-GATHER_X_FIRST = (True, True, False, True)
-SCATTER_X_FIRST = (False, False, False, True)
 ORDER = (
-    ("U", 0), ("W", 0), ("X", 0), ("Y0", 0), ("Y2", 0), ("U", 3), ("K", 0), ("Y3", 0), ("Y1", 0), ("F0", 0),
-    ("X", 3), ("Y2", 3), ("U", 2), ("Y0", 3), ("F1", 0), ("U", 1), ("C", 0), ("Y1", 3), ("Y3", 3), ("y0", 2),
-    ("x0", 2), ("X", 1), ("F0", 3), ("Y2", 1), ("R1", 0), ("Y0", 1), ("x1", 2), ("F1", 3), ("f0", 2), ("C", 3),
-    ("Y1", 1), ("Y3", 1), ("x2", 2), ("R2a", 0), ("x3", 2), ("R2b", 0), ("R1", 3), ("C", 2), ("F0", 1), ("F1", 1),
-    ("r2", 3), ("R3", 0), ("R1", 2), ("C", 1), ("r3", 3), ("R2a", 2), ("R2b", 2), ("R1", 1), ("R4", 0), ("R4", 3),
-    ("Z", 0), ("R3", 2), ("R2a", 1), ("R2b", 1), ("R4", 2), ("R3", 1), ("Z", 3), ("R4", 1), ("Z", 2), ("Z", 1),
+    ("K", 0), ("W", 0), ("U", 0), ("D", 0), ("D", 1), ("D", 2), ("X", 0), ("Y0", 0), ("U", 3), ("D", 3),
+    ("Y1", 0), ("D", 4), ("U", 2), ("X", 3), ("D", 5), ("U", 1), ("Y0", 3), ("C1", 0), ("Y0", 2), ("D", 6),
+    ("C2", 0), ("Y1", 3), ("X", 2), ("D", 7), ("Y0", 1), ("X", 1), ("C1", 3), ("Y1", 2), ("C2", 3), ("Y1", 1),
+    ("R1", 0), ("C1", 2), ("R1", 3), ("C2", 2), ("C1", 1), ("R4", 0), ("C2", 1), ("R1", 2), ("R4", 3), ("Z", 0),
+    ("R1", 1), ("R4", 2), ("R4", 1), ("Z", 3), ("Z", 2), ("Z", 1),
 )
 
 
@@ -78,23 +75,24 @@
 def kernel(
     tokens_hbm, ids_hbm, gate_hbm, gain_hbm, w_gate, w_up, w_down, out,
     tokens, ids, gate_weight, gain,
-    pack, arrived, blocks, wide, down, down_raw, hidden, core_out, core_in, sums, partial_in, x_out,
-    back, returned, picks, total0, total1,
-    in_sem, w_sem, z_send, z_recv, g_send, g_x, g_y, g_core, p_send, p_recv, r_send, r_recv,
-    b_send, b_recv,
+    pack, arrived, blocks, wide, wide_peer, down, down_raw, down4, half_own, half_out, half_in, hidden,
+    sums, partial_in, back, returned, picks, total0, total1,
+    in_sem, w_sem, v_send, v_recv, d_send, d_recv, z_send, z_recv, g_send, g_x, g_y, p_send, p_recv,
+    h_send, h_recv, r_send, r_recv, b_send, b_recv,
 ):
     section, expert = lax.axis_index("section"), lax.axis_index("expert")
     xl, y, core = section // 8, (section // 2) % 4, section % 2
     xh, z = expert // 16, expert % 16
     up, dn, far = (y + 1) % 4, (y + 3) % 4, (y + 2) % 4
     ox = 1 - xl
-    onward, behind = jnp.where(core == 0, up, dn), jnp.where(core == 0, dn, up)
+    corner = xl * 2 + core
 
     def sec(a, b, c):
         return ((a * 4 + b) * 2 + c, expert)
 
     to_x, to_up, to_dn, to_core = sec(ox, y, core), sec(xl, up, core), sec(xl, dn, core), sec(xl, y, 1 - core)
-    to_onward = sec(xl, onward, core)
+    to_far, to_diagonal = sec(xl, far, core), sec(ox, y, 1 - core)
+    partners = ((to_core, xl, 1 - core), (to_x, ox, core), (to_diagonal, ox, 1 - core))
 
     inputs = []
     for j, (src, dst) in enumerate(((ids_hbm, ids), (tokens_hbm, tokens), (gain_hbm, gain), (gate_hbm, gate_weight))):
@@ -114,7 +112,7 @@
         load.start()
 
     barrier = pltpu.get_barrier_semaphore()
-    for peer in (to_core, to_x, to_up, to_dn):
+    for peer in (to_core, to_x, to_diagonal, to_up, to_dn, to_far):
         pl.semaphore_signal(barrier, inc=1, device_id=peer, device_id_type=MESH)
 
     @pl.loop(1, 32)
@@ -154,7 +152,7 @@
     arrived[0] = pack[0]
     gain_row = dot(jnp.broadcast_to(gain[...], (16, FEAT)), widen)[0:1, :]
 
-    pl.semaphore_wait(barrier, 35)
+    pl.semaphore_wait(barrier, 37)
 
     for q in SEND_ORDER:
 
@@ -185,6 +183,7 @@
         wide[:, FEAT:LANES, :] = jnp.zeros((16, LANES - FEAT, LANES), BF16)
         for load in loads:
             load.wait()
+        send(wide.at[pl.ds((1 - core) * 8, 8)], wide_peer, v_send, v_recv, to_core)
         for s in range(16):
             first = (s * FEAT) // 128 * 128
             shift = s * FEAT - first
@@ -192,19 +191,23 @@
             place = (s % 2) * 8 + s // 2
             down[place, :, 0:FEAT] = window.astype(F32)[:, shift : shift + FEAT].astype(BF16)
             down[place, :, FEAT:LANES] = jnp.zeros((128, LANES - FEAT), BF16)
+        for b in range(4):
+            down4[b, corner] = down[core * 8 + chip(xl, b)]
+            give_down(0, b)
+
+    def give_down(j, b):
+        peer, a, c = partners[j]
+        send(down.at[c * 8 + chip(a, b)], down4.at[b, corner], d_send, d_recv.at[j], peer)
 
     def chip(a, b):
         return a * 4 + b
 
-    def block(q, a, b, c):
-        return blocks.at[q, c * 8 + chip(a, b)]
-
     def share(q, a, b, peer, recv_sem):
-        ref = block(q, a, b, core)
+        ref = blocks.at[q, chip(a, b)]
         send(ref, ref, g_send.at[q], recv_sem, peer)
 
-    def to_peer(q, a, b):
-        share(q, a, b, to_core, g_core.at[q])
+    def await_block(q, a, b, sem):
+        await_bytes(blocks.at[q, chip(a, b)], sem)
 
     def unpack(q):
         skip = 1 if q == 0 else 0
@@ -224,115 +227,78 @@
         x = jnp.where(lane == FEAT, high, x)
         x = jnp.where(lane == FEAT + 1, mid, x)
         x = jnp.where(lane == FEAT + 2, low, x)
-        blocks[q, core * 8 + chip(xl, y)] = x.astype(BF16)
-        share(q, xl, y, to_x, g_x.at[q, 0])
+        blocks[q, chip(xl, y)] = x.astype(BF16)
+        share(q, xl, y, to_x, g_x.at[q])
         share(q, xl, y, to_up, g_y.at[q, 0])
         share(q, xl, y, to_dn, g_y.at[q, 1])
-        to_peer(q, xl, y)
-
-    def x_then_y(q):
-        await_bytes(block(q, ox, y, core), g_x.at[q, 0])
+
+    def relay_x(q):
+        await_block(q, ox, y, g_x.at[q])
         share(q, ox, y, to_up, g_y.at[q, 2])
         share(q, ox, y, to_dn, g_y.at[q, 3])
-        to_peer(q, ox, y)
 
     def relay_up(q):
-        await_bytes(block(q, xl, dn, core), g_y.at[q, 0])
+        await_block(q, xl, dn, g_y.at[q, 0])
         share(q, xl, dn, to_up, g_y.at[q, 4])
-        to_peer(q, xl, dn)
 
     def relay_dn(q):
-        await_bytes(block(q, ox, up, core), g_y.at[q, 3])
+        await_block(q, ox, up, g_y.at[q, 3])
         share(q, ox, up, to_dn, g_y.at[q, 5])
-        to_peer(q, ox, up)
-
-    def keep(q, a, b, sem):
-        await_bytes(block(q, a, b, core), sem)
-        to_peer(q, a, b)
-
-    def y_then_x(q):
-        await_bytes(block(q, xl, dn, core), g_y.at[q, 0])
-        await_bytes(block(q, xl, up, core), g_y.at[q, 1])
-        share(q, xl, behind, to_onward, g_y.at[q, 2])
-        share(q, xl, dn, to_x, g_x.at[q, 1])
-        share(q, xl, up, to_x, g_x.at[q, 2])
-        to_peer(q, xl, dn)
-        to_peer(q, xl, up)
-
-    def far_then_x(q):
-        await_bytes(block(q, xl, far, core), g_y.at[q, 2])
-        share(q, xl, far, to_x, g_x.at[q, 3])
-        to_peer(q, xl, far)
-
-    def compute(q):
-        await_bytes(blocks.at[q, pl.ds((1 - core) * 8, 8)], g_core.at[q])
-        product = jnp.zeros((ROWS, LANES), F32)
+
+    waited = set()
+
+    def once(name, wait):
+        if name not in waited:
+            waited.add(name)
+            wait()
+
+    def contract(q):
+        await_block(q, xl, up, g_y.at[q, 1])
+        await_block(q, ox, dn, g_y.at[q, 2])
+        await_block(q, xl, far, g_y.at[q, 4])
+        await_block(q, ox, far, g_y.at[q, 5])
+        once("wide", lambda: await_bytes(wide_peer, v_recv))
+        own = jnp.zeros((ROWS, LANES), F32)
+        other = jnp.zeros((ROWS, LANES), F32)
         squares = jnp.zeros((ROWS, 128), F32)
-        for k in range(16):
+        for k in range(8):
             x = blocks[q, k]
-            product = product + dot(x, wide[k])
+            own = own + dot(x, wide[core * 8 + k])
+            other = other + dot(x, wide_peer[k])
             squares = squares + x[:, 128:256].astype(F32)
+        half_out[q, :, 0:LANES] = other
+        half_out[q, :, LANES : LANES + 128] = squares
+        send(half_out.at[q], half_in.at[q], p_send.at[q], p_recv.at[q], to_core)
+        half_own[q, :, 0:LANES] = own
+        half_own[q, :, LANES : LANES + 128] = squares
+
+    def activate(q):
+        await_bytes(half_in.at[q], p_recv.at[q])
+        both = half_own[q] + half_in[q]
         lane = iota((ROWS, 128), 1)
         kept = (lane >= FEAT - 128) & (lane < FEAT - 128 + 3)
-        square = jnp.sum(jnp.where(kept, squares, 0.0), axis=1, keepdims=True)
+        square = jnp.sum(jnp.where(kept, both[:, LANES : LANES + 128], 0.0), axis=1, keepdims=True)
         scale = lax.rsqrt(square * (1.0 / D) + epsilon)
-        gate, upward = product[:, 0:128] * scale, product[:, 128:256] * scale
-        hidden[q] = (gate / (1.0 + jnp.exp(-gate)) * upward).astype(BF16)
-        for k in range(8):
-            core_out[q, k] = dot(hidden[q], down[(1 - core) * 8 + k]).astype(BF16)
-        send(core_out.at[q], core_in.at[q], p_send.at[q], p_recv.at[q], to_core)
-
-    def pass_on(q, place, j, peer):
-        send(sums.at[q, place], partial_in.at[q, j], r_send.at[q], r_recv.at[q, j], peer)
-
-    def take(q, j):
-        await_bytes(partial_in.at[q, j], r_recv.at[q, j])
-        return partial_in[q, j].astype(F32)
-
-    def add_core(q):
-        await_bytes(core_in.at[q], p_recv.at[q])
-        for k in range(8):
-            own = dot(hidden[q], down[core * 8 + k])
-            sums[q, k] = (own + core_in[q, k].astype(F32)).astype(BF16)
-        if SCATTER_X_FIRST[q]:
-            for j, b in enumerate((far, up, dn, y)):
-                pass_on(q, chip(ox, b), j, to_x)
-        else:
-            pass_on(q, chip(xl, far), 0, to_up)
-            pass_on(q, chip(ox, far), 1, to_dn)
-            pass_on(q, chip(ox, up), 2, to_up)
-            pass_on(q, chip(xl, dn), 3, to_dn)
-
-    def add_into(q, place, j):
-        sums[q, place] = (sums[q, place].astype(F32) + take(q, j)).astype(BF16)
-
-    def far_up(q):
-        add_into(q, chip(xl, up), 0)
-        pass_on(q, chip(xl, up), 4, to_up)
-
-    def far_dn(q):
-        add_into(q, chip(ox, dn), 1)
-        pass_on(q, chip(ox, dn), 5, to_dn)
-
-    def y_sum(q):
-        x_out[q] = (sums[q, chip(ox, y)].astype(F32) + take(q, 2) + take(q, 5)).astype(BF16)
-        send(x_out.at[q], partial_in.at[q, 6], r_send.at[q], r_recv.at[q, 6], to_x)
-
-    def x_far(q):
-        add_into(q, chip(xl, far), 0)
-        pass_on(q, chip(xl, far), 4, to_onward)
-
-    def x_near(q):
-        add_into(q, chip(xl, up), 1)
-        add_into(q, chip(xl, dn), 2)
-        add_into(q, chip(xl, onward), 4)
-        pass_on(q, chip(xl, up), 5, to_up)
-        pass_on(q, chip(xl, dn), 6, to_dn)
+        gate, upward = both[:, 0:128] * scale, both[:, 128:256] * scale
+        hidden[q, corner] = (gate / (1.0 + jnp.exp(-gate)) * upward).astype(BF16)
+        for j in (2, 1, 0):
+            send(hidden.at[q, corner], hidden.at[q, corner], h_send.at[q], h_recv.at[q, j], partners[j][0])
+
+    def spread_out(q):
+        for j, (_, a, c) in enumerate(partners):
+            await_bytes(hidden.at[q, a * 2 + c], h_recv.at[q, j])
+            once(j, lambda: await_bytes(down4.at[:, a * 2 + c], d_recv.at[j]))
+        units = jnp.concatenate([hidden[q, k] for k in range(4)], axis=1)
+        for j, (b, peer) in enumerate(((far, to_far), (up, to_up), (dn, to_dn), (y, None))):
+            sums[q, j] = dot(units, down4[b].reshape(512, LANES)).astype(BF16)
+            if peer is not None:
+                send(sums.at[q, j], partial_in.at[q, j], r_send.at[q], r_recv.at[q, j], peer)
 
     def finish(q):
-        total = sums[q, chip(xl, y)].astype(F32)
-        for j in (3, 5, 6) if SCATTER_X_FIRST[q] else (3, 4, 6):
-            total = total + take(q, j)
+        total = sums[q, 3].astype(F32)
+        for j in (1, 2, 0):
+            await_bytes(partial_in.at[q, j], r_recv.at[q, j])
+            total = total + partial_in[q, j].astype(F32)
         row, col = iota((MAIN, 2 * PER), 0), iota((MAIN, 2 * PER), 1)
         slot = row % 16
         spread = one_hot((row // 16 == col // 2) & (slot < 14) & ((slot >= 7).astype(I32) == col % 2))
@@ -358,16 +324,9 @@
 
     tasks = {
         "W": prepare_weights, "K": prepare_mix,
-        "U": unpack, "C": compute, "R1": add_core, "R4": finish, "Z": mix,
-        "X": x_then_y, "Y0": relay_up, "Y1": relay_dn,
-        "Y2": lambda q: keep(q, xl, up, g_y.at[q, 1]), "Y3": lambda q: keep(q, ox, dn, g_y.at[q, 2]),
-        "F0": lambda q: keep(q, xl, far, g_y.at[q, 4]), "F1": lambda q: keep(q, ox, far, g_y.at[q, 5]),
-        "y0": y_then_x, "f0": far_then_x,
-        "x0": lambda q: keep(q, ox, y, g_x.at[q, 0]),
-        "x1": lambda q: keep(q, ox, dn, g_x.at[q, 1]),
-        "x2": lambda q: keep(q, ox, up, g_x.at[q, 2]),
-        "x3": lambda q: keep(q, ox, far, g_x.at[q, 3]),
-        "R2a": far_up, "R2b": far_dn, "R3": y_sum, "r2": x_far, "r3": x_near,
+        "U": unpack, "X": relay_x, "Y0": relay_up, "Y1": relay_dn,
+        "C1": contract, "C2": activate, "R1": spread_out, "R4": finish, "Z": mix,
+        "D": lambda i: give_down(2 - i % 2, i // 2),
     }
     for name, q in ORDER:
         tasks[name](q)
@@ -378,10 +337,13 @@
 
     await_bytes(pack.at[pl.ds(1, 31)], z_send)
     await_bytes(back.at[pl.ds(1, 31)], b_send)
+    await_bytes(wide_peer, v_send)
+    await_bytes(down.at[pl.ds(0, 12)], d_send)
     for q in range(GROUPS):
-        await_bytes(blocks.at[q, pl.ds(0, 15)], g_send.at[q])
-        await_bytes(core_out.at[q], p_send.at[q])
-        await_bytes(partial_in.at[q], r_send.at[q])
+        await_bytes(blocks.at[q, pl.ds(0, 7)], g_send.at[q])
+        await_bytes(half_out.at[q], p_send.at[q])
+        await_bytes(hidden.at[q, pl.ds(0, 3)], h_send.at[q])
+        await_bytes(sums.at[q, pl.ds(0, 3)], r_send.at[q])
 
 
 def on_device(tokens, norm_gain, expert_ids, gate_weight, w_gate, w_up, w_down):
@@ -399,26 +361,26 @@
             pltpu.VMEM((1, FEAT), BF16),
             pltpu.VMEM((32, 16, LANES), BF16),
             pltpu.VMEM((32, 16, LANES), BF16),
-            pltpu.VMEM((GROUPS, 16) + block, BF16),
+            pltpu.VMEM((GROUPS, 8) + block, BF16),
             pltpu.VMEM((16, LANES, LANES), BF16),
+            pltpu.VMEM((8, LANES, LANES), BF16),
             pltpu.VMEM((16, 128, LANES), BF16),
             pltpu.VMEM((128, D), BF16),
-            pltpu.VMEM((GROUPS, ROWS, 128), BF16),
-            pltpu.VMEM((GROUPS, 8) + block, BF16),
-            pltpu.VMEM((GROUPS, 8) + block, BF16),
-            pltpu.VMEM((GROUPS, 8) + block, BF16),
-            pltpu.VMEM((GROUPS, 7) + block, BF16),
-            pltpu.VMEM((GROUPS,) + block, BF16),
+            pltpu.VMEM((4, 4, 128, LANES), BF16),
+            pltpu.VMEM((GROUPS, ROWS, LANES + 128), F32),
+            pltpu.VMEM((GROUPS, ROWS, LANES + 128), F32),
+            pltpu.VMEM((GROUPS, ROWS, LANES + 128), F32),
+            pltpu.VMEM((GROUPS, 4, ROWS, 128), BF16),
+            pltpu.VMEM((GROUPS, 4) + block, BF16),
+            pltpu.VMEM((GROUPS, 3) + block, BF16),
             pltpu.VMEM((32, 16, LANES), BF16),
             pltpu.VMEM((32, 16, LANES), BF16),
             pltpu.VMEM((GROUPS, 2, 2 * TOK, MAIN), BF16),
             pltpu.VMEM((TOK, LANES), F32),
             pltpu.VMEM((TOK, LANES), F32),
-            dma((4,)), dma((5,)), dma, dma((GROUPS,)),
-            dma((GROUPS,)), dma((GROUPS, 4)), dma((GROUPS, 6)), dma((GROUPS,)),
-            dma((GROUPS,)), dma((GROUPS,)),
-            dma((GROUPS,)), dma((GROUPS, 7)),
-            dma, dma((GROUPS,)),
+            dma((4,)), dma((5,)), dma, dma, dma, dma((3,)), dma, dma((GROUPS,)),
+            dma((GROUPS,)), dma((GROUPS,)), dma((GROUPS, 6)), dma((GROUPS,)), dma((GROUPS,)),
+            dma((GROUPS,)), dma((GROUPS, 3)), dma((GROUPS,)), dma((GROUPS, 3)), dma, dma((GROUPS,)),
         ],
         compiler_params=pltpu.CompilerParams(
             collective_id=0, has_side_effects=True, vmem_limit_bytes=60 * 1024 * 1024

time: 85.3 us -> 78 us (0.914)
  Pallas kernels: 83.3 us -> 76.4 us
    pallas_call x1, Pallas kernels: 83.3 us -> 76.4 us  [on_device(): pl.pallas_call(kernel, out_shape=jax.ShapeDtypeStruct((TOK, FEAT), BF16),...]
where the time goes in v4:
time: 78 us; the launch traced here: 77.9 us
  Pallas kernels  76.4 us (98%)
  local copies, waits for them, and re-layouts  1.52 us (2%)
    pallas_call x1, Pallas kernels, on_device(): pl.pallas_call(kernel, out_shape=jax.ShapeDtypeStruct((TOK, FEAT), BF16),...  76.4 us

profile of v4, /device:TPU:6, one launch (start us, length us, event | category | flops | bytes accessed | tf_op | source)
XLA Modules:
  0.0 77.9 jit_solution(6082458536333071283)
XLA Ops:
  0.0 76.4 %shard_map.73 = bf16[144,224]{1,0:T(8,128)(2,1)} custom-call(bf16[144,224]{1,0:T(8,128)(2,1)} %tokens_hbm.1, s32[2,144]{1,0:T(2,128)} %bitcast.8, f32[2,144]{1,0:T(2,128)} %bitcast.9, bf16[1,224]{1,0:T(2,128)(2,1)} %gain_hbm.1, bf16[8,2,224,128]{3,2,1,0:T(8,128)(2,1)} %bitcast.5, bf16[8,2,224,128]{3,2,1,0:T(8,128)(2,1)} %bitcast.6, bf16[128,3584]{1,0:T(8,128)(2,1)} %bitcast.7), custom_call_target="tpu_custom_call" | custom-call | flops 2000000000 | bytes 3000000 | tf_op jit(solution)/shard_map/pallas_call | solution.py:352
  76.4 1.5 %copy.9 = bf16[144,224]{1,0:T(8,128)(2,1)} copy(bf16[144,224]{1,0:T(8,128)(2,1)} %shard_map.73) | data formatting | bytes 129024

commit v5 on v4

--- a/solution.py
+++ b/solution.py
@@ -19,13 +19,14 @@
 BF16 = jnp.bfloat16
 I32 = jnp.int32
 MESH = pl.DeviceIdType.MESH
-SEND_ORDER = (0, 3, 2, 1)
+NEAR_ORDER = (0, 1)
+FAR_ORDER = (3, 2)
 ORDER = (
-    ("K", 0), ("W", 0), ("U", 0), ("D", 0), ("D", 1), ("D", 2), ("X", 0), ("Y0", 0), ("U", 3), ("D", 3),
-    ("Y1", 0), ("D", 4), ("U", 2), ("X", 3), ("D", 5), ("U", 1), ("Y0", 3), ("C1", 0), ("Y0", 2), ("D", 6),
-    ("C2", 0), ("Y1", 3), ("X", 2), ("D", 7), ("Y0", 1), ("X", 1), ("C1", 3), ("Y1", 2), ("C2", 3), ("Y1", 1),
-    ("R1", 0), ("C1", 2), ("R1", 3), ("C2", 2), ("C1", 1), ("R4", 0), ("C2", 1), ("R1", 2), ("R4", 3), ("Z", 0),
-    ("R1", 1), ("R4", 2), ("R4", 1), ("Z", 3), ("Z", 2), ("Z", 1),
+    ("W", 0), ("K", 0), ("D", 4), ("D", 1), ("D", 6), ("S", 0), ("U", 0), ("U", 1), ("D", 5), ("D", 3),
+    ("X", 0), ("D", 0), ("X", 1), ("Y1", 0), ("Y0", 1), ("Y1", 1), ("U", 3), ("Y0", 0), ("U", 2), ("C1", 1),
+    ("Y0", 3), ("X", 3), ("C2", 1), ("D", 7), ("X", 2), ("Y0", 2), ("Y1", 3), ("D", 2), ("Y1", 2), ("C1", 3),
+    ("R1", 1), ("C2", 3), ("C1", 2), ("C2", 2), ("R1", 3), ("R4", 1), ("C1", 0), ("R1", 2), ("C2", 0), ("R4", 3),
+    ("Z", 1), ("R1", 0), ("R4", 2), ("R4", 0), ("Z", 3), ("Z", 0), ("Z", 2),
 )
 
 
@@ -78,7 +79,7 @@
     pack, arrived, blocks, wide, wide_peer, down, down_raw, down4, half_own, half_out, half_in, hidden,
     sums, partial_in, back, returned, picks, total0, total1,
     in_sem, w_sem, v_send, v_recv, d_send, d_recv, z_send, z_recv, g_send, g_x, g_y, p_send, p_recv,
-    h_send, h_recv, r_send, r_recv, b_send, b_recv,
+    h_send, h_recv, r_send, r_recv, b_send, b_recv, near_sem,
 ):
     section, expert = lax.axis_index("section"), lax.axis_index("expert")
     xl, y, core = section // 8, (section // 2) % 4, section % 2
@@ -115,7 +116,7 @@
     for peer in (to_core, to_x, to_diagonal, to_up, to_dn, to_far):
         pl.semaphore_signal(barrier, inc=1, device_id=peer, device_id_type=MESH)
 
-    @pl.loop(1, 32)
+    @pl.loop(1, 18)
     def _(place):
         pl.semaphore_signal(
             barrier, inc=1, device_id=(section, peer_expert(place, xh, z, 1)), device_id_type=MESH
@@ -152,16 +153,26 @@
     arrived[0] = pack[0]
     gain_row = dot(jnp.broadcast_to(gain[...], (16, FEAT)), widen)[0:1, :]
 
-    pl.semaphore_wait(barrier, 37)
-
-    for q in SEND_ORDER:
-
+    pl.semaphore_wait(barrier, 23)
+    for step in (4, 12):
+        quarter = (section, xh * 16 + (z + step) % 16)
+        pl.semaphore_signal(near_sem, inc=1, device_id=quarter, device_id_type=MESH)
+
+    def dispatch(q):
         @pl.loop(q * PER + (1 if q == 0 else 0), q * PER + PER)
         def _(place):
             send(
                 pack.at[place], arrived.at[place], z_send, z_recv.at[q],
                 (section, peer_expert(place, xh, z, -1)),
             )
+
+    def dispatch_far(_):
+        pl.semaphore_wait(near_sem, 2)
+        for q in FAR_ORDER:
+            dispatch(q)
+
+    for q in NEAR_ORDER:
+        dispatch(q)
 
     def column_of(line):
         same = iota((TOK, TOK), 0) == iota((TOK, TOK), 1)
@@ -323,7 +334,7 @@
         total1[...] += picked[TOK : 2 * TOK]
 
     tasks = {
-        "W": prepare_weights, "K": prepare_mix,
+        "S": dispatch_far, "W": prepare_weights, "K": prepare_mix,
         "U": unpack, "X": relay_x, "Y0": relay_up, "Y1": relay_dn,
         "C1": contract, "C2": activate, "R1": spread_out, "R4": finish, "Z": mix,
         "D": lambda i: give_down(2 - i % 2, i // 2),
@@ -381,6 +392,7 @@
             dma((4,)), dma((5,)), dma, dma, dma, dma((3,)), dma, dma((GROUPS,)),
             dma((GROUPS,)), dma((GROUPS,)), dma((GROUPS, 6)), dma((GROUPS,)), dma((GROUPS,)),
             dma((GROUPS,)), dma((GROUPS, 3)), dma((GROUPS,)), dma((GROUPS, 3)), dma, dma((GROUPS,)),
+            pltpu.SemaphoreType.REGULAR,
         ],
         compiler_params=pltpu.CompilerParams(
             collective_id=0, has_side_effects=True, vmem_limit_bytes=60 * 1024 * 1024

time: 78 us -> 75.6 us (0.969)
  the two profiles are of different devices: /device:TPU:6 before, /device:TPU:8 now
where the time goes in v5:
time: 75.6 us; the launch traced here: 75.4 us
  Pallas kernels  73.9 us (98%)
  local copies, waits for them, and re-layouts  1.52 us (2%)
    pallas_call x1, Pallas kernels, on_device(): pl.pallas_call(kernel, out_shape=jax.ShapeDtypeStruct((TOK, FEAT), BF16),...  73.9 us
    unnamed x1, local copies, waits for them, and re-layouts  1.52 us

profile of v5, /device:TPU:8, one launch (start us, length us, event | category | flops | bytes accessed | tf_op | source)
XLA Modules:
  0.0 75.4 jit_solution(7895490005437454150)
XLA Ops:
  0.0 73.9 %shard_map.73 = bf16[144,224]{1,0:T(8,128)(2,1)} custom-call(bf16[144,224]{1,0:T(8,128)(2,1)} %tokens_hbm.1, s32[2,144]{1,0:T(2,128)} %bitcast.8, f32[2,144]{1,0:T(2,128)} %bitcast.9, bf16[1,224]{1,0:T(2,128)(2,1)} %gain_hbm.1, bf16[8,2,224,128]{3,2,1,0:T(8,128)(2,1)} %bitcast.5, bf16[8,2,224,128]{3,2,1,0:T(8,128)(2,1)} %bitcast.6, bf16[128,3584]{1,0:T(8,128)(2,1)} %bitcast.7), custom_call_target="tpu_custom_call" | custom-call | flops 2000000000 | bytes 3000000 | tf_op jit(solution)/shard_map/pallas_call | solution.py:363
  73.9 1.5 %copy.9 = bf16[144,224]{1,0:T(8,128)(2,1)} copy(bf16[144,224]{1,0:T(8,128)(2,1)} %shard_map.73) | data formatting | bytes 129024

commit v6 on v5

--- a/solution.py
+++ b/solution.py
@@ -21,12 +21,13 @@
 MESH = pl.DeviceIdType.MESH
 NEAR_ORDER = (0, 1)
 FAR_ORDER = (3, 2)
+FAR_RELAY = (True, True, False, False)
 ORDER = (
-    ("W", 0), ("K", 0), ("D", 4), ("D", 1), ("D", 6), ("S", 0), ("U", 0), ("U", 1), ("D", 5), ("D", 3),
-    ("X", 0), ("D", 0), ("X", 1), ("Y1", 0), ("Y0", 1), ("Y1", 1), ("U", 3), ("Y0", 0), ("U", 2), ("C1", 1),
-    ("Y0", 3), ("X", 3), ("C2", 1), ("D", 7), ("X", 2), ("Y0", 2), ("Y1", 3), ("D", 2), ("Y1", 2), ("C1", 3),
-    ("R1", 1), ("C2", 3), ("C1", 2), ("C2", 2), ("R1", 3), ("R4", 1), ("C1", 0), ("R1", 2), ("C2", 0), ("R4", 3),
-    ("Z", 1), ("R1", 0), ("R4", 2), ("R4", 0), ("Z", 3), ("Z", 0), ("Z", 2),
+    ("S", 0), ("W", 0), ("U", 0), ("U", 1), ("D", 3), ("X", 0), ("Y0", 0), ("D", 5), ("X", 1), ("D", 4),
+    ("Y1", 0), ("Y1", 1), ("D", 0), ("Y0", 1), ("U", 3), ("D", 7), ("D", 1), ("D", 2), ("X", 3), ("C1", 1),
+    ("U", 2), ("C2", 1), ("C1", 0), ("X", 2), ("D", 6), ("C2", 0), ("C1", 3), ("K", 0), ("C2", 3), ("R1", 1),
+    ("C1", 2), ("R1", 3), ("C2", 2), ("R4", 1), ("R1", 2), ("R4", 3), ("Z", 1), ("R1", 0), ("R4", 2), ("R4", 0),
+    ("Z", 3), ("Z", 0), ("Z", 2),
 )
 
 
@@ -45,7 +46,7 @@
 def peer_expert(place, xh, z, sign):
     step = place // 2
     half = (step + 1) // 2
-    offset = half * (2 * (step % 2) - 1)
+    offset = half * (2 * (step % 2) - 1) * (1 - 2 * (place % 2))
     return ((xh + place % 2) % 2) * 16 + (z + sign * offset + 16) % 16
 
 
@@ -242,11 +243,15 @@
         share(q, xl, y, to_x, g_x.at[q])
         share(q, xl, y, to_up, g_y.at[q, 0])
         share(q, xl, y, to_dn, g_y.at[q, 1])
+        if not FAR_RELAY[q]:
+            share(q, xl, y, to_far, g_y.at[q, 4])
 
     def relay_x(q):
         await_block(q, ox, y, g_x.at[q])
         share(q, ox, y, to_up, g_y.at[q, 2])
         share(q, ox, y, to_dn, g_y.at[q, 3])
+        if not FAR_RELAY[q]:
+            share(q, ox, y, to_far, g_y.at[q, 5])
 
     def relay_up(q):
         await_block(q, xl, dn, g_y.at[q, 0])
@@ -264,6 +269,9 @@
             wait()
 
     def contract(q):
+        if not FAR_RELAY[q]:
+            await_block(q, xl, dn, g_y.at[q, 0])
+            await_block(q, ox, up, g_y.at[q, 3])
         await_block(q, xl, up, g_y.at[q, 1])
         await_block(q, ox, dn, g_y.at[q, 2])
         await_block(q, xl, far, g_y.at[q, 4])

time: 75.6 us -> 72 us (0.952)
  the two profiles are of different devices: /device:TPU:8 before, /device:TPU:6 now
where the time goes in v6:
time: 72 us; the launch traced here: 71.2 us
  Pallas kernels  69.7 us (97%)
  local copies, waits for them, and re-layouts  1.52 us (2%)
    pallas_call x1, Pallas kernels, on_device(): pl.pallas_call(kernel, out_shape=jax.ShapeDtypeStruct((TOK, FEAT), BF16),...  69.7 us
    unnamed x1, local copies, waits for them, and re-layouts  1.52 us

profile of v6, /device:TPU:6, one launch (start us, length us, event | category | flops | bytes accessed | tf_op | source)
XLA Modules:
  0.0 71.2 jit_solution(13505021986696836250)
XLA Ops:
  0.0 69.7 %shard_map.73 = bf16[144,224]{1,0:T(8,128)(2,1)} custom-call(bf16[144,224]{1,0:T(8,128)(2,1)} %tokens_hbm.1, s32[2,144]{1,0:T(2,128)} %bitcast.8, f32[2,144]{1,0:T(2,128)} %bitcast.9, bf16[1,224]{1,0:T(2,128)(2,1)} %gain_hbm.1, bf16[8,2,224,128]{3,2,1,0:T(8,128)(2,1)} %bitcast.5, bf16[8,2,224,128]{3,2,1,0:T(8,128)(2,1)} %bitcast.6, bf16[128,3584]{1,0:T(8,128)(2,1)} %bitcast.7), custom_call_target="tpu_custom_call" | custom-call | flops 2000000000 | bytes 3000000 | tf_op jit(solution)/shard_map/pallas_call | solution.py:371
  69.7 1.5 %copy.9 = bf16[144,224]{1,0:T(8,128)(2,1)} copy(bf16[144,224]{1,0:T(8,128)(2,1)} %shard_map.73) | data formatting | bytes 129024

commit v7 on v6

--- a/solution.py
+++ b/solution.py
@@ -21,13 +21,13 @@
 MESH = pl.DeviceIdType.MESH
 NEAR_ORDER = (0, 1)
 FAR_ORDER = (3, 2)
-FAR_RELAY = (True, True, False, False)
+MODES = "xxXX"
 ORDER = (
-    ("S", 0), ("W", 0), ("U", 0), ("U", 1), ("D", 3), ("X", 0), ("Y0", 0), ("D", 5), ("X", 1), ("D", 4),
-    ("Y1", 0), ("Y1", 1), ("D", 0), ("Y0", 1), ("U", 3), ("D", 7), ("D", 1), ("D", 2), ("X", 3), ("C1", 1),
-    ("U", 2), ("C2", 1), ("C1", 0), ("X", 2), ("D", 6), ("C2", 0), ("C1", 3), ("K", 0), ("C2", 3), ("R1", 1),
-    ("C1", 2), ("R1", 3), ("C2", 2), ("R4", 1), ("R1", 2), ("R4", 3), ("Z", 1), ("R1", 0), ("R4", 2), ("R4", 0),
-    ("Z", 3), ("Z", 0), ("Z", 2),
+    ("W", 0), ("S", 3), ("U", 0), ("U", 1), ("D", 3), ("X", 0), ("Y0", 0), ("D", 5), ("X", 1), ("S", 2),
+    ("D", 4), ("Y1", 0), ("Y1", 1), ("D", 0), ("Y0", 1), ("U", 3), ("D", 7), ("D", 1), ("D", 2), ("X", 3),
+    ("C1", 1), ("U", 2), ("C2", 1), ("C1", 0), ("X", 2), ("D", 6), ("C2", 0), ("C1", 3), ("K", 0), ("C2", 3),
+    ("R1", 1), ("C1", 2), ("R1", 3), ("C2", 2), ("R4", 1), ("R1", 2), ("R4", 3), ("Z", 1), ("R1", 0), ("R4", 2),
+    ("R4", 0), ("Z", 3), ("Z", 0), ("Z", 2),
 )
 
 
@@ -167,10 +167,10 @@
                 (section, peer_expert(place, xh, z, -1)),
             )
 
-    def dispatch_far(_):
-        pl.semaphore_wait(near_sem, 2)
-        for q in FAR_ORDER:
-            dispatch(q)
+    def dispatch_far(q):
+        if q == FAR_ORDER[0]:
+            pl.semaphore_wait(near_sem, 2)
+        dispatch(q)
 
     for q in NEAR_ORDER:
         dispatch(q)
@@ -243,15 +243,34 @@
         share(q, xl, y, to_x, g_x.at[q])
         share(q, xl, y, to_up, g_y.at[q, 0])
         share(q, xl, y, to_dn, g_y.at[q, 1])
-        if not FAR_RELAY[q]:
+        if MODES[q] != "x":
             share(q, xl, y, to_far, g_y.at[q, 4])
 
-    def relay_x(q):
+    def relay_to_y(q):
         await_block(q, ox, y, g_x.at[q])
         share(q, ox, y, to_up, g_y.at[q, 2])
         share(q, ox, y, to_dn, g_y.at[q, 3])
-        if not FAR_RELAY[q]:
+        if MODES[q] != "x":
             share(q, ox, y, to_far, g_y.at[q, 5])
+
+    def relay_to_x(q):
+        for j, (b, onward) in enumerate(((dn, 2), (up, 3), (far, 5))):
+            await_block(q, xl, b, g_y.at[q, (0, 1, 4)[j]])
+            share(q, xl, b, to_x, g_y.at[q, onward])
+
+    def await_column(q):
+        for b, sem in ((dn, 0), (up, 1), (far, 4)):
+            await_block(q, xl, b, g_y.at[q, sem])
+
+    def by_core(first, second):
+        pl.when(core == 0)(first)
+        pl.when(core == 1)(second)
+
+    def relay(q):
+        if MODES[q] == "M":
+            by_core(lambda: relay_to_y(q), lambda: relay_to_x(q))
+        else:
+            relay_to_y(q)
 
     def relay_up(q):
         await_block(q, xl, dn, g_y.at[q, 0])
@@ -269,12 +288,17 @@
             wait()
 
     def contract(q):
-        if not FAR_RELAY[q]:
-            await_block(q, xl, dn, g_y.at[q, 0])
+        if MODES[q] == "x":
+            await_block(q, xl, up, g_y.at[q, 1])
+            await_block(q, ox, dn, g_y.at[q, 2])
+            await_block(q, xl, far, g_y.at[q, 4])
+        else:
+            if MODES[q] == "X":
+                await_column(q)
+            else:
+                by_core(lambda: await_column(q), lambda: await_block(q, ox, y, g_x.at[q]))
+            await_block(q, ox, dn, g_y.at[q, 2])
             await_block(q, ox, up, g_y.at[q, 3])
-        await_block(q, xl, up, g_y.at[q, 1])
-        await_block(q, ox, dn, g_y.at[q, 2])
-        await_block(q, xl, far, g_y.at[q, 4])
         await_block(q, ox, far, g_y.at[q, 5])
         once("wide", lambda: await_bytes(wide_peer, v_recv))
         own = jnp.zeros((ROWS, LANES), F32)
@@ -343,7 +367,7 @@
 
     tasks = {
         "S": dispatch_far, "W": prepare_weights, "K": prepare_mix,
-        "U": unpack, "X": relay_x, "Y0": relay_up, "Y1": relay_dn,
+        "U": unpack, "X": relay, "Y0": relay_up, "Y1": relay_dn,
         "C1": contract, "C2": activate, "R1": spread_out, "R4": finish, "Z": mix,
         "D": lambda i: give_down(2 - i % 2, i // 2),
     }

time: 72 us -> 71.7 us (level)
  no operation moved by 1% of the time
where the time goes in v7:
time: 71.7 us; the launch traced here: 70.8 us
  Pallas kernels  69.3 us (97%)
  local copies, waits for them, and re-layouts  1.52 us (2%)
    pallas_call x1, Pallas kernels, on_device(): pl.pallas_call(kernel, out_shape=jax.ShapeDtypeStruct((TOK, FEAT), BF16),...  69.3 us
    unnamed x1, local copies, waits for them, and re-layouts  1.52 us

profile of v7, /device:TPU:6, one launch (start us, length us, event | category | flops | bytes accessed | tf_op | source)
XLA Modules:
  0.0 70.8 jit_solution(12673849079523862339)
XLA Ops:
  0.0 69.3 %shard_map.73 = bf16[144,224]{1,0:T(8,128)(2,1)} custom-call(bf16[144,224]{1,0:T(8,128)(2,1)} %tokens_hbm.1, s32[2,144]{1,0:T(2,128)} %bitcast.8, f32[2,144]{1,0:T(2,128)} %bitcast.9, bf16[1,224]{1,0:T(2,128)(2,1)} %gain_hbm.1, bf16[8,2,224,128]{3,2,1,0:T(8,128)(2,1)} %bitcast.5, bf16[8,2,224,128]{3,2,1,0:T(8,128)(2,1)} %bitcast.6, bf16[128,3584]{1,0:T(8,128)(2,1)} %bitcast.7), custom_call_target="tpu_custom_call" | custom-call | flops 2000000000 | bytes 3000000 | tf_op jit(solution)/shard_map/pallas_call | solution.py:395
  69.3 1.5 %copy.9 = bf16[144,224]{1,0:T(8,128)(2,1)} copy(bf16[144,224]{1,0:T(8,128)(2,1)} %shard_map.73) | data formatting | bytes 129024

commit v8 on v7

--- a/solution.py
+++ b/solution.py
@@ -23,9 +23,9 @@
 FAR_ORDER = (3, 2)
 MODES = "xxXX"
 ORDER = (
-    ("W", 0), ("S", 3), ("U", 0), ("U", 1), ("D", 3), ("X", 0), ("Y0", 0), ("D", 5), ("X", 1), ("S", 2),
-    ("D", 4), ("Y1", 0), ("Y1", 1), ("D", 0), ("Y0", 1), ("U", 3), ("D", 7), ("D", 1), ("D", 2), ("X", 3),
-    ("C1", 1), ("U", 2), ("C2", 1), ("C1", 0), ("X", 2), ("D", 6), ("C2", 0), ("C1", 3), ("K", 0), ("C2", 3),
+    ("W", 0), ("K", 0), ("S", 3), ("U", 0), ("U", 1), ("D", 3), ("X", 0), ("Y0", 0), ("D", 5), ("X", 1),
+    ("S", 2), ("D", 4), ("Y1", 0), ("Y1", 1), ("D", 0), ("Y0", 1), ("U", 3), ("D", 7), ("D", 1), ("D", 2),
+    ("X", 3), ("C1", 1), ("U", 2), ("C2", 1), ("C1", 0), ("X", 2), ("D", 6), ("C2", 0), ("C1", 3), ("C2", 3),
     ("R1", 1), ("C1", 2), ("R1", 3), ("C2", 2), ("R4", 1), ("R1", 2), ("R4", 3), ("Z", 1), ("R1", 0), ("R4", 2),
     ("R4", 0), ("Z", 3), ("Z", 0), ("Z", 2),
 )
@@ -376,7 +376,7 @@
 
     weights = [column_of(gate_weight[k : k + 1, :]) for k in range(2)]
     mixed = weights[0] * total0[...] + weights[1] * total1[...]
-    out[...] = mixed[:, 0:FEAT].astype(BF16)
+    out[...] = mixed
 
     await_bytes(pack.at[pl.ds(1, 31)], z_send)
     await_bytes(back.at[pl.ds(1, 31)], b_send)
@@ -392,9 +392,9 @@
 def on_device(tokens, norm_gain, expert_ids, gate_weight, w_gate, w_up, w_down):
     dma = pltpu.SemaphoreType.DMA
     block = (ROWS, LANES)
-    return pl.pallas_call(
+    mixed = pl.pallas_call(
         kernel,
-        out_shape=jax.ShapeDtypeStruct((TOK, FEAT), BF16),
+        out_shape=jax.ShapeDtypeStruct((TOK, LANES), F32),
         in_specs=[pl.BlockSpec(memory_space=pl.ANY)] * 7,
         out_specs=pl.BlockSpec(memory_space=pltpu.VMEM),
         scratch_shapes=[
@@ -434,6 +434,7 @@
         tokens, expert_ids.T, gate_weight.T, norm_gain,
         w_gate.reshape(8, 2, FEAT, 128), w_up.reshape(8, 2, FEAT, 128), w_down[0],
     )
+    return mixed[:, 0:FEAT].astype(BF16)
 
 
 def solution(mesh):

time: 71.7 us -> 71.8 us (level)
    slice x0 -> x1, local copies, waits for them, and re-layouts: none -> 1.55 us  [on_device(): return mixed[:, 0:FEAT].astype(BF16)]
    unnamed x1 -> x0, local copies, waits for them, and re-layouts: 1.52 us -> none
where the time goes in v8:
time: 71.8 us; the launch traced here: 70.8 us
  Pallas kernels  69.2 us (96%)
  local copies, waits for them, and re-layouts  1.55 us (2%)
    pallas_call x1, Pallas kernels, on_device(): pl.pallas_call(kernel, out_shape=jax.ShapeDtypeStruct((TOK, LANES), F32),...  69.2 us
    slice x1, local copies, waits for them, and re-layouts, on_device(): return mixed[:, 0:FEAT].astype(BF16)  1.55 us

profile of v8, /device:TPU:6, one launch (start us, length us, event | category | flops | bytes accessed | tf_op | source)
XLA Modules:
  0.0 70.8 jit_solution(8952101727793978581)
XLA Ops:
  0.0 69.2 %shard_map.73 = f32[144,256]{1,0:T(8,128)} custom-call(bf16[144,224]{1,0:T(8,128)(2,1)} %tokens_hbm.1, s32[2,144]{1,0:T(2,128)} %bitcast.8, f32[2,144]{1,0:T(2,128)} %bitcast.9, bf16[1,224]{1,0:T(2,128)(2,1)} %gain_hbm.1, bf16[8,2,224,128]{3,2,1,0:T(8,128)(2,1)} %bitcast.5, bf16[8,2,224,128]{3,2,1,0:T(8,128)(2,1)} %bitcast.6, bf16[128,3584]{1,0:T(8,128)(2,1)} %bitcast.7), custom_call_target="tpu_custom_call" | custom-call | flops 2000000000 | bytes 3000000 | tf_op jit(solution)/shard_map/pallas_call | solution.py:395
  69.2 1.6 %slice.7 = bf16[144,224]{1,0:T(8,128)(2,1)} slice(f32[144,256]{1,0:T(8,128)} %shard_map.73), slice={[0:144], [0:224]} | slice | bytes 129024 | tf_op jit(solution)/shard_map/slice | solution.py:437
